TPU v7x, 128 devices: a whole 4x4x4 slice. The times are simulated.
128 devices in a mesh: gx: 8 (over x, z_hi), gy: 4 (over z_lo, core), gz: 4 (over y).
Axes of the slice: x: 4, y: 4, z: 4 (z_hi: 2, z_lo: 2; z = z_hi * 2 + z_lo), core: 2. Of those that a mesh axis runs over, the one named last changes fastest.
Arguments:
- rhs_field: float32 [192, 128, 1024], P('gz', 'gy', 'gx'), may hold values from -24 to 24
- stiffness: float32 [192, 128, 1024], P('gz', 'gy', 'gx'), may hold values from 0.03 to 0.3
Outputs:
- solution: float32 [192, 128, 1024], P('gz', 'gy', 'gx')
- residual: float32 [192, 128, 1024], P('gz', 'gy', 'gx')
All inputs are finite; a program needn't handle non-finite values.
Results may differ from a plain program's by a relative error of at most 0.0015.
Values sent between devices are 32-bit elements; how exact they have to be, the bound alone decides.
No kernel may reach another device: no remote copies, remote signals or barrier semaphores. Data moves between devices by JAX's collectives and lax.ppermute only.
A program may use at most 128 MiB of HBM per device.

v0:
```python
import functools

import jax
import jax.numpy as jnp
import numpy as np
from jax import lax
from jax.experimental import pallas as pl
from jax.experimental.pallas import tpu as pltpu
from jax.sharding import PartitionSpec as P

OV = 4
ITERS = 3
CZ, CY, CX = 48, 32, 128
EZ, EY, EX = CZ + 2 * OV, CY + 2 * OV, CX + 2 * OV
UZ, UY, UX = CZ + 12, 48, 256
GROUP = 4
TABLES = 7
CHUNK = 2
INNER = [(z, 4) for z in range(10, 46, 4)]
OUTER = [(0, 6), (6, 4), (46, 6), (52, 4)]


class Shape:
    def __init__(self, last):
        self.rim = 6 if last else 10
        self.halo = 4 if last else 6
        self.width = 4 + self.halo
        self.per = 128 // self.width
        self.x_tiles = -(-EZ // self.per) * 5
        self.x_groups = self.x_tiles // 5
        self.extra_a = EZ if last else EZ + EZ // 4
        self.extra_b = self.extra_a + -(-EZ // 16)
        self.y_tiles = self.extra_b + (0 if last else 1)
        self.cut_near = 4 if last else 2
        self.c_tiles = 2 * self.x_groups + (0 if last else -(-self.x_groups // 2))
        self.last = last


mass_term = 1e-05
split_term = 0.5
bend_mean = 0.1
f32, bf16 = jnp.float32, jnp.bfloat16


def sine_table(length):
    places = np.arange(1, length + 1, dtype=np.float64)
    return np.sqrt(2.0 / (length + 1)) * np.sin(
        np.pi * places[:, None] * places[None, :] / (length + 1)
    )


def eigen_line(length):
    places = np.arange(1, length + 1, dtype=np.float64)
    return 2.0 - 2.0 * np.cos(np.pi * places / (length + 1))


def halves(table):
    high = np.asarray(table, np.float32).astype(jnp.bfloat16)
    low = (np.asarray(table, np.float64) - high.astype(np.float64)).astype(jnp.bfloat16)
    return [jnp.asarray(high), jnp.asarray(low)]


def solve_tables():
    column = np.zeros((UX, UX))
    full = sine_table(EX)
    for lane in range(UX):
        place = lane + OV if lane < CX + OV else lane - UX + OV
        if 0 <= place < EX:
            column[lane, :EX] = full[place]
    rows = np.roll(sine_table(EY), -OV, axis=0)
    row_fwd = np.kron(np.eye(2), rows.T)
    spectrum = (
        eigen_line(EZ)[None, :, None]
        + eigen_line(EY)[:, None, None]
        + eigen_line(EX)[None, None, :]
    )
    inverse = np.zeros((EY, EZ, UX), np.float32)
    inverse[:, :, :EX] = 1.0 / (mass_term + bend_mean * spectrum**2 + split_term * spectrum)
    tables = []
    for table in (column, column.T):
        tables += halves(table)
    for table in (row_fwd, row_fwd.T, sine_table(EZ)):
        high, low = halves(table)
        tables.append(jnp.concatenate([high, low, high], axis=1))
    return tables + [jnp.asarray(inverse)]


def cut(values):
    high = values.astype(bf16)
    return high, (values - high.astype(f32)).astype(bf16)


def mul(a, b):
    return lax.dot_general(a, b, (((1,), (0,)), ((), ())), preferred_element_type=f32)


def mul3(a, b):
    return mul(a[0], b[0]) + (mul(a[0], b[1]) + mul(a[1], b[0]))


def lanes():
    return lax.broadcasted_iota(jnp.int32, (8, 128), 1)


def subs():
    return lax.broadcasted_iota(jnp.int32, (8, 128), 0)


def spin(values, shift, axis):
    size = values.shape[axis]
    shift = shift % size
    return values if shift == 0 else pltpu.roll(values, shift, axis)


def pack(into, values, lead, width, at):
    lane = lax.broadcasted_iota(jnp.int32, values.shape, 1)
    inside = (lane >= width * at) & (lane < width * (at + 1))
    moved = spin(values, lead + width * at, 1)
    return jnp.where(inside, moved, 0.0 if into is None else into)


def unpack(packed, lead, width, at):
    moved = spin(packed, -(lead + width * at), 1)
    lane = lax.broadcasted_iota(jnp.int32, packed.shape, 1)
    return jnp.where((lane >= 128 - lead) | (lane < width - lead), moved, 0.0)


class Later:
    def __init__(self):
        self.kept = []

    def put(self, ref, index, values):
        self.kept.append((ref, index, values))

    def flush(self):
        for ref, index, values in self.kept:
            ref[index] = values
        self.kept = []


def row_product(table, values):
    out, step = [], 2 * EY
    for at in range(0, values.shape[0], step):
        high, low = cut(values[at : at + step])
        out.append(mul(table, jnp.concatenate([high, high, low], axis=0)))
    return jnp.concatenate(out, axis=0)


def depth_product(table, values):
    high = values.astype(bf16).astype(f32)
    return mul(table, jnp.concatenate([high, high, values - high], axis=0).astype(bf16))


def forward(values, tables, later, parts, z):
    count = values.shape[0] * EY
    values = mul3(cut(values.reshape(count, UX)), (tables[0][...], tables[1][...]))
    values = row_product(tables[4][...], values)
    later.flush()
    for side in (0, 1):
        columns = slice(128 * side, 128 * side + 128)
        later.put(parts[side], slice(z * EY, z * EY + count), values[:, columns])


def finish_solve(parts, solved, tables, inverse, shape, low, high):
    column, row, depth = (tables[2][...], tables[3][...]), tables[5][...], tables[6][...]
    for b in range(EY):
        rows = pl.ds(b, EZ, stride=EY)
        values = jnp.concatenate([parts[0][rows, :], parts[1][rows, :]], axis=1)
        values = depth_product(depth, depth_product(depth, values) * inverse[b])
        parts[0][rows, :] = values[:, :CX]
        parts[1][rows, :] = values[:, CX:]

    later = Later()
    for z in range(0, EZ, GROUP):
        rows = slice(z * EY, (z + GROUP) * EY)
        values = jnp.concatenate([parts[0][rows, :], parts[1][rows, :]], axis=1)
        values = mul3(cut(row_product(row, values)), column).reshape(GROUP, EY, UX)
        later.flush()
        later.put(solved, slice(z, z + GROUP), values)
    later.flush()

    lane = lanes()
    for first in range(0, EZ, shape.per):
        for tile in range(5):
            rows = slice(8 * tile, 8 * tile + 8)
            packed = [None, None]
            for j in range(min(shape.per, EZ - first)):
                near, far = solved[first + j, rows, :CX], solved[first + j, rows, CX:]
                packed[0] = pack(
                    packed[0], jnp.where(lane >= 124, far, near), OV, shape.width, j
                )
                packed[1] = pack(
                    packed[1],
                    jnp.where(lane >= 128 - shape.halo, near, far),
                    shape.halo,
                    shape.width,
                    j,
                )
            low[first // shape.per * 5 + tile] = packed[0]
            high[first // shape.per * 5 + tile] = packed[1]


def column_folded(solved, from_left, from_right, shape, z, tile):
    lane, rows = lanes(), slice(8 * tile, 8 * tile + 8)
    at, j = z // shape.per * 5 + tile, z % shape.per
    left = unpack(from_left[at], shape.halo, shape.width, j)
    right = unpack(from_right[at], OV, shape.width, j)
    return (
        solved[z, rows, :CX] + jnp.where(lane < 64, left, right),
        solved[z, rows, CX:] + jnp.where(lane < 64, right, left),
    )


def row_strips_kernel(shape, solved, low, high):
    sub = subs()
    for strip, cut_at, upper, lower, keep in (
        (low, 4, 4, 0, 4),
        (high, shape.cut_near, 3, 4, 2),
    ):
        extra_a = extra_b = None
        for quad in range(EZ // 4):
            rest = [None, None]
            for j in range(4):
                z = 4 * quad + j
                for side in (0, 1):
                    columns = slice(128 * side, 128 * side + 128)
                    lower_tile = solved[z, 8 * lower : 8 * lower + 8, columns]
                    upper_tile = solved[z, 8 * upper : 8 * upper + 8, columns]
                    main = jnp.where(sub >= cut_at, upper_tile, lower_tile)
                    if side == 0:
                        strip[z] = main
                    else:
                        extra_a = pack(extra_a if z % 16 else None, main, OV, 2 * OV, z % 16)
                        if z % 16 == 15 or z + 1 == EZ:
                            strip[shape.extra_a + z // 16] = extra_a
                    if not shape.last:
                        inside = (sub >= 2 * j) & (sub < 2 * j + 2)
                        moved = spin(lower_tile, 2 * j - keep, 0)
                        rest[side] = jnp.where(inside, moved, rest[side] if j else 0.0)
            if not shape.last:
                strip[EZ + quad] = rest[0]
                extra_b = pack(extra_b, rest[1], OV, 2 * OV, quad)
        if not shape.last:
            strip[shape.extra_b] = extra_b


def corners_kernel(shape, from_left, from_right, low, high):
    sub, groups = subs(), shape.x_groups
    for strip, cut_at, upper, lower, keep in (
        (low, 4, 4, 0, 4),
        (high, shape.cut_near, 3, 4, 2),
    ):
        rest = None
        for k in range(2 * groups):
            source = (from_left, from_right)[k // groups]
            lower_tile = source[k % groups * 5 + lower]
            strip[k] = jnp.where(sub >= cut_at, source[k % groups * 5 + upper], lower_tile)
            if shape.last:
                continue
            j = k % 4
            inside = (sub >= 2 * j) & (sub < 2 * j + 2)
            rest = jnp.where(inside, spin(lower_tile, 2 * j - keep, 0), rest if j else 0.0)
            if j == 3 or k + 1 == 2 * groups:
                strip[2 * groups + k // 4] = rest


def widen_kernel(shape, solved, from_left, from_right, folded):
    sub = subs()
    for z in range(EZ):
        for tile in range(5):
            values = column_folded(solved, from_left, from_right, shape, z, tile)
            for side in (0, 1):
                columns = slice(128 * side, 128 * side + 128)
                value = values[side]
                if tile == 4:
                    folded[z, 40:48, columns] = jnp.where(sub >= 4, value, 0.0)
                    value = jnp.where(sub < 4, value, 0.0)
                folded[z, 8 * tile : 8 * tile + 8, columns] = value


def row_part(strip, shape, z, side, keep):
    sub = subs()
    if side == 0:
        main = strip[z]
    else:
        main = unpack(strip[shape.extra_a + z // 16], OV, 2 * OV, z % 16)
    if shape.last:
        return main, jnp.zeros((8, 128), f32)
    if side == 0:
        rest = strip[EZ + z // 4]
    else:
        rest = unpack(strip[shape.extra_b], OV, 2 * OV, z // 4)
    moved = spin(rest, keep - 2 * (z % 4), 0)
    return main, jnp.where((sub >= keep) & (sub < keep + 2), moved, 0.0)


def depth_strips_kernel(
    shape, widened, from_near, from_far, corner_near, corner_far, folded, low, high, corners
):
    sub, lane, cut_at = subs(), lanes(), shape.cut_near
    groups = shape.x_groups
    for k in range(2 * groups):
        for strip, keep in ((corner_near, 2), (corner_far, 4)):
            main, rest = strip[k], 0.0
            if not shape.last:
                moved = spin(strip[2 * groups + k // 4], keep - 2 * (k % 4), 0)
                rest = jnp.where((sub >= keep) & (sub < keep + 2), moved, 0.0)
            if keep == 2:
                corners[0, k] = jnp.where(sub < cut_at, main, rest)
                corners[1, k] = jnp.where(sub >= cut_at, main, 0.0)
            else:
                corners[2, k] = jnp.where(sub >= 4, main, 0.0)
                corners[3, k] = jnp.where(sub < 4, main, rest)
    for z in range(EZ):
        group, j = z // shape.per, z % shape.per
        new = {}
        for side in (0, 1):
            main, rest = row_part(from_near, shape, z, side, 2)
            new[0, side] = jnp.where(sub < cut_at, main, rest)
            new[5, side] = jnp.where(sub >= cut_at, main, 0.0)
            main, rest = row_part(from_far, shape, z, side, 4)
            new[3, side] = jnp.where(sub >= 4, main, 0.0)
            new[4, side] = jnp.where(sub < 4, main, rest)
        for at, tile in enumerate((0, 5, 3, 4)):
            left = unpack(corners[at, group], shape.halo, shape.width, j)
            right = unpack(corners[at, groups + group], OV, shape.width, j)
            new[tile, 0] += jnp.where(lane < 64, left, right)
            new[tile, 1] += jnp.where(lane < 64, right, left)
        for side in (0, 1):
            columns = slice(128 * side, 128 * side + 128)
            for tile in range(6):
                rows = slice(8 * tile, 8 * tile + 8)
                value = widened[z, rows, columns]
                if (tile, side) in new:
                    value = value + new[tile, side]
                folded[z, rows, columns] = value
    for strip, start in ((low, 0), (high, EZ - shape.rim)):
        extra = None
        for i in range(shape.rim):
            strip[i] = folded[start + i, :, :CX]
            extra = pack(extra, folded[start + i, :, CX:], shape.halo, 2 * shape.halo, i)
        strip[shape.rim] = extra


def laplace(below, centre, above):
    beside = below + above
    beside = beside + (pltpu.roll(centre, 1, 0) + pltpu.roll(centre, UY - 1, 0))
    beside = beside + (pltpu.roll(centre, 1, 1) + pltpu.roll(centre, UX - 1, 1))
    return 6.0 * centre - beside


def operate(get, shift, span, flux, weighted, stiffness, wide, core, unroll):
    start, stop = span

    def chunks(body, start, stop, carry):
        size = CHUNK
        while (stop - start) % size:
            size -= 1
        return lax.fori_loop(
            0,
            (stop - start) // size,
            lambda i, c: body(start + size * i, size, c),
            carry,
            unroll=unroll,
        )

    def first(at, size, carry):
        later = Later()
        for z in [at + i for i in range(size)]:
            values = laplace(get(z - 1), get(z), get(z + 1))
            later.put(flux, z - shift, values)
            later.put(weighted, z - shift, stiffness[z] * values)
        later.flush()
        return carry

    chunks(first, start - 1, stop + 1, 0)
    sub = lax.broadcasted_iota(jnp.int32, (8, UX), 0)

    def second(base, size, carry, use_core):
        later = Later()
        for z in [base + i for i in range(size)]:
            own = get(z)
            at = z - shift
            values = laplace(weighted[at - 1], weighted[at], weighted[at + 1])
            values = mass_term * own + values + split_term * flux[at]
            if wide is not None:
                later.put(wide, (z - 2, slice(0, CY)), values[:CY])
                last = jnp.where(sub < 4, values[CY : CY + 8], values[CY + 8 :])
                later.put(wide, (z - 2, slice(CY, EY)), last)
            if use_core:
                carry = core(z, own[:CY, :CX], values[:CY, :CX], carry, later)
        later.flush()
        return carry

    return lambda first_z, last_z, carry, use_core: chunks(
        lambda z, size, c: second(z, size, c, use_core), first_z, last_z, carry
    )


def add_up(total, product):
    return total + ((product[0:8] + product[8:16]) + (product[16:24] + product[24:32]))


def core_step(count, rhs, earlier, smooth, image):
    def step(z, own, core, totals, later):
        at = z - 6
        later.put(smooth, at, own)
        later.put(image, at, core)
        new = [add_up(totals[0], own * rhs[at])]
        for i in range(count):
            new.append(add_up(totals[1 + i], core * earlier[i][at]))
        new.append(add_up(totals[1 + count], core * own))
        return tuple(new)

    return step


def inner_kernel(count, shape, *refs):
    folded, stiffness, rhs = refs[:3]
    earlier, refs = refs[3 : 3 + count], refs[3 + count :]
    tables = ()
    if not shape.last:
        tables, refs = refs[:TABLES], refs[TABLES:]
    smooth, image, sums = refs[:3]
    wide, halves_out = (None, None) if shape.last else (refs[-3], refs[3:5])
    flux, weighted = refs[-2:]
    step = core_step(count, rhs, earlier, smooth, image)
    run = operate(
        lambda z: folded[z - 2], 10, (12, 48), flux, weighted, stiffness, wide, step, 6
    )
    totals = run(12, 48, (jnp.zeros((8, 128), f32),) * (count + 2), True)
    for i, value in enumerate(totals):
        sums[i] = value
    if not shape.last:
        later = Later()
        for z, layers in INNER:
            forward(wide[z : z + layers], tables, later, halves_out, z)
        later.flush()


def outer_kernel(count, shape, *refs):
    folded, from_below, from_above, stiffness, rhs = refs[:5]
    earlier, refs = refs[5 : 5 + count], refs[5 + count :]
    smooth_in, image_in, sums_in = refs[:3]
    refs = refs[3:]
    wide = None
    if shape.last:
        parts, refs = refs[:count], refs[count:]
    else:
        halves_in, inverse = refs[:2], refs[2]
        tables, refs = refs[3 : 3 + TABLES], refs[3 + TABLES :]
        wide, halves_out = refs[-4], refs[-6:-4]
    smooth, image, sums = refs[:3]
    full, flux, weighted = refs[-3:]
    smooth[6:42] = smooth_in[6:42]
    image[6:42] = image_in[6:42]
    edge = 10 - shape.rim
    step = core_step(count, rhs, earlier, smooth, image)
    totals = tuple(sums_in[i] for i in range(count + 2))
    first_z = 6 if shape.last else 2
    for strip, base, shift in ((from_below, edge, 0), (from_above, 50, 46)):
        for z in range(14):
            layer = z + shift
            if not (4 if shape.last else 0) <= layer < (56 if shape.last else 60):
                continue
            at = layer - base
            inside = 2 <= layer < UZ - 2
            if 0 <= at < shape.rim:
                extra = unpack(strip[shape.rim], shape.halo, 2 * shape.halo, at)
                if inside:
                    full[z, :, :CX] = folded[layer - 2, :, :CX] + strip[at]
                    full[z, :, CX:] = folded[layer - 2, :, CX:] + extra
                else:
                    full[z, :, :CX] = strip[at]
                    full[z, :, CX:] = extra
            else:
                full[z] = folded[layer - 2]
        span = (first_z, 12) if shift == 0 else (48, UZ - first_z)
        run = operate(
            lambda z, shift=shift: full[z - shift],
            shift,
            span,
            flux,
            weighted,
            stiffness,
            wide,
            step,
            2,
        )
        if shift == 0:
            if not shape.last:
                run(2, 6, 0, False)
            totals = run(6, 12, totals, True)
        else:
            totals = run(48, 54, totals, True)
            if not shape.last:
                run(54, 58, 0, False)
    if not shape.last:
        for i, value in enumerate(totals):
            sums[i] = value
        solved, low, high = refs[3:6]
        for part, source in zip(halves_out, halves_in):
            part[10 * EY : 46 * EY] = source[10 * EY : 46 * EY]
        later = Later()
        for z, layers in OUTER:
            forward(wide[z : z + layers], tables, later, halves_out, z)
        later.flush()
        finish_solve(
            halves_out, solved, tables, inverse, Shape(count + 2 == ITERS), low, high
        )
        return
    lane = lanes()
    values = [part[i] for part in parts for i in range(part.shape[0])] + list(totals)
    gathered = jnp.zeros((8, 128), f32)
    for i, value in enumerate(values):
        value = jnp.sum(jnp.sum(value, axis=0, keepdims=True), axis=1, keepdims=True)
        gathered = jnp.where(lane == i, value, gathered)
    sums[...] = gathered


def start_columns_kernel(rhs, stiffness, low, high):
    for source, base, width in ((rhs, 0, 4), (stiffness, 8, 5)):
        per = 128 // width
        for first in range(0, CZ, per):
            for tile in range(4):
                packed = [None, None]
                for j in range(min(per, CZ - first)):
                    values = source[first + j, 8 * tile : 8 * tile + 8, :]
                    packed[0] = pack(packed[0], values, 0, width, j)
                    packed[1] = pack(packed[1], values, width, width, j)
                low[base + first // per * 4 + tile] = packed[0]
                high[base + first // per * 4 + tile] = packed[1]


def ends(left, right, width, j):
    lane = lanes()
    left = spin(left, -(width + width * j), 1)
    right = spin(right, -width * j, 1)
    return jnp.where(lane >= 128 - width, left, jnp.where(lane < width, right, 0.0))


def start_extra(from_left, from_right, base, width, z, tile):
    per = 128 // width
    at = base + z // per * 4 + tile
    return ends(from_left[at], from_right[at], width, z % per)


START_RHS, START_ST, START_ONE, START_Y = 0, 24, 48, 54


def start_rows_kernel(rhs, stiffness, low, high):
    sub = subs()
    strips = ((low, 0), (high, 3))

    def pairing(k, carry):
        for source, main_at in ((rhs, START_RHS), (stiffness, START_ST)):
            for strip, tile in strips:
                rows = slice(8 * tile, 8 * tile + 8)
                a, b = source[2 * k, rows, :], source[2 * k + 1, rows, :]
                if tile == 0:
                    strip[main_at + k] = jnp.where(sub < 4, a, spin(b, 4, 0))
                else:
                    strip[main_at + k] = jnp.where(sub < 4, spin(a, -4, 0), b)
        return carry

    lax.fori_loop(0, CZ // 2, pairing, 0, unroll=4)

    def single(k, carry):
        for strip, tile in strips:
            row = jnp.zeros((8, 128), f32)
            for j in range(8):
                values = stiffness[8 * k + j, 8 * tile : 8 * tile + 8, :]
                moved = spin(values, j - (4 if tile == 0 else 3), 0)
                row = jnp.where(sub == j, moved, row)
            strip[START_ONE + k] = row
        return carry

    lax.fori_loop(0, CZ // 8, single, 0, unroll=2)


def start_corners_kernel(from_left, from_right, low, high):
    for strip, tile in ((low, 0), (high, 3)):
        for group in range(4):
            strip[group] = from_left[4 * group + tile]
            strip[4 + group] = from_right[4 * group + tile]


def start_depth_kernel(
    rhs,
    stiffness,
    from_left,
    from_right,
    from_near,
    from_far,
    corner_near,
    corner_far,
    wide,
    stiff,
    low,
    high,
):
    sub = subs()

    def corner(strip, first, width, z):
        per = 128 // width
        at = first + z // per
        return ends(strip[at], strip[4 + at], width, z % per)

    for z in range(CZ):
        for tile in range(4):
            rows = slice(8 * tile, 8 * tile + 8)
            wide[z, rows, :CX] = rhs[z, rows, :]
            stiff[z + 6, rows, :CX] = stiffness[z, rows, :]
            wide[z, rows, CX:] = start_extra(from_left, from_right, 0, 4, z, tile)
            stiff[z + 6, rows, CX:] = start_extra(from_left, from_right, 8, 5, z, tile)
        odd = z % 2
        far, near = from_far[START_RHS + z // 2], from_near[START_RHS + z // 2]
        far, near = (spin(far, 4, 0), near) if odd else (far, spin(near, 4, 0))
        wide[z, 32:40, :CX] = jnp.where(sub < 4, far, near)
        far, near = corner(corner_far, 0, 4, z), corner(corner_near, 0, 4, z)
        wide[z, 32:40, CX:] = jnp.where(sub < 4, far, near)
        far, near = from_far[START_ST + z // 2], from_near[START_ST + z // 2]
        far, near = (spin(far, 4, 0), near) if odd else (far, spin(near, 4, 0))
        one = spin(from_far[START_ONE + z // 8], 4 - z % 8, 0)
        stiff[z + 6, 32:40, :CX] = jnp.where(sub < 4, far, jnp.where(sub == 4, one, 0.0))
        one = spin(from_near[START_ONE + z // 8], 3 - z % 8, 0)
        stiff[z + 6, 40:48, :CX] = jnp.where(sub >= 4, near, jnp.where(sub == 3, one, 0.0))
        far, near = corner(corner_far, 2, 5, z), corner(corner_near, 2, 5, z)
        stiff[z + 6, 32:40, CX:] = jnp.where(sub <= 4, far, 0.0)
        stiff[z + 6, 40:48, CX:] = jnp.where(sub >= 3, near, 0.0)
    blank = jnp.zeros((8, 128), f32)
    for strip, wide_at, stiff_at in ((low, 0, 6), (high, CZ - 4, CZ + 1)):
        extra = None
        for i in range(4):
            strip[i, :40] = wide[wide_at + i, :, :CX]
            strip[i, 40:48] = blank
        for i in range(5):
            strip[4 + i] = stiff[stiff_at + i, :, :CX]
            extra = pack(extra, stiff[stiff_at + i, :, CX:], 5, 10, i)
        strip[9] = extra
        for tile in range(5):
            rows = slice(8 * tile, 8 * tile + 8)
            extra = strip[9, rows, :]
            for i in range(4):
                lane = lanes()
                moved = spin(wide[wide_at + i, rows, CX:], 4 + 64 + 8 * i, 1)
                inside = (lane >= 64 + 8 * i) & (lane < 72 + 8 * i)
                extra = jnp.where(inside, moved, extra)
            strip[9, rows, :] = extra


def start_inner_kernel(wide, *refs):
    tables, halves_out = refs[:TABLES], refs[TABLES:]
    later = Later()
    for z in range(4, 52, GROUP):
        forward(wide[z - 4 : z], tables, later, halves_out, z)
    later.flush()


def start_outer_kernel(from_below, from_above, stiff_in, *refs):
    halves_in, inverse = refs[:2], refs[2]
    tables, refs = refs[3 : 3 + TABLES], refs[3 + TABLES :]
    solved, stiff, low, high, edge = refs[:5]
    halves_out, later = refs[5:], Later()
    for part, source in zip(halves_out, halves_in):
        part[4 * EY : 52 * EY] = source[4 * EY : 52 * EY]
    stiff[6:54] = stiff_in[6:54]
    for strip, first, stiff_at in ((from_below, 0, 1), (from_above, 52, 54)):
        lane = lax.broadcasted_iota(jnp.int32, (EY, CX), 1)
        for i in range(4):
            edge[i, :, :CX] = strip[i, :40]
            moved = spin(strip[9, :40], -(4 + 64 + 8 * i), 1)
            edge[i, :, CX:] = jnp.where((lane >= 124) | (lane < 4), moved, 0.0)
        for i in range(5):
            stiff[stiff_at + i, :, :CX] = strip[4 + i]
            stiff[stiff_at + i, :, CX:] = unpack(strip[9], 5, 10, i)
        forward(edge[...], tables, later, halves_out, first)
        later.flush()
    finish_solve(halves_out, solved, tables, inverse, Shape(False), low, high)


def weights(b, pair):
    sigma = [jnp.zeros((1, 1), f32)] * ITERS
    delta = None
    current = None
    for turn in range(ITERS):
        zeta = [jnp.ones((1, 1), f32)] + [-s for s in sigma[:turn]]
        following = sum(z * b[i] for i, z in enumerate(zeta))
        for i, z in enumerate(zeta):
            for j in range(turn):
                following = following - z * sigma[j] * pair[i, j]
        if turn == 0:
            delta = zeta
        else:
            ratio = following / current
            delta = [z + ratio * d for z, d in zip(zeta, delta + [jnp.zeros((1, 1), f32)])]
        current = following
        bending = sum(
            delta[i] * delta[j] * pair[i, j] for i in range(turn + 1) for j in range(turn + 1)
        )
        step = current / bending
        sigma = [
            s + step * d for s, d in zip(sigma, delta + [jnp.zeros((1, 1), f32)] * (ITERS - turn - 1))
        ]
    return sigma


def combine_kernel(sums, rhs, u0, u1, u2, w0, w1, w2, answer, rest):
    picked = [
        jnp.sum(jnp.where(lanes()[:1] == i, sums[:1], 0.0), axis=1, keepdims=True)
        for i in range(ITERS * (ITERS + 3) // 2)
    ]
    b, pair, at = [], {}, 0
    for j in range(ITERS):
        b.append(picked[at])
        for i in range(j + 1):
            pair[i, j] = pair[j, i] = picked[at + 1 + i]
        at += j + 2
    s = weights(b, pair)

    def step(z, carry):
        answer[z] = s[0] * u0[z] + s[1] * u1[z] + s[2] * u2[z]
        rest[z] = rhs[z] - (s[0] * w0[z] + s[1] * w1[z] + s[2] * w2[z])
        return carry

    lax.fori_loop(0, CZ, step, 0, unroll=4)


VMEM = pl.BlockSpec(memory_space=pltpu.VMEM)


def call(kernel, shapes, operands, scratch=(), cost=2.0):
    return pl.pallas_call(
        kernel,
        out_shape=[jax.ShapeDtypeStruct(shape, f32) for shape in shapes],
        in_specs=[VMEM] * len(operands),
        out_specs=[VMEM] * len(shapes),
        scratch_shapes=[pltpu.VMEM(shape, f32) for shape in scratch],
        cost_estimate=pl.CostEstimate(
            flops=int(cost * 1e9), bytes_accessed=int(cost * 3.6e6), transcendentals=0
        ),
        compiler_params=pltpu.CompilerParams(vmem_limit_bytes=20 * 2**20),
    )(*operands)


def shifted(block, axis, step):
    count = lax.axis_size(axis)
    return lax.ppermute(block, axis, [(i, (i + step) % count) for i in range(count)])


def swap(low, high, axis):
    return shifted(high, axis, 1), shifted(low, axis, -1)


def ring(values, axes, count, low, size):
    parts = []
    for step in range(1, size):
        route = []
        for i in range(count):
            place = i // low % size
            route.append((i, i + ((place + step) % size - place) * low))
        parts.append(lax.ppermute(values, axes, route))
    return values + sum(parts[1:], parts[0])


def total(values):
    values = ring(values, "gy", 4, 1, 2)
    values = ring(values, ("gx", "gy"), 32, 2, 4)
    values = ring(values, "gx", 8, 2, 4)
    return ring(values, "gz", 4, 1, 4)


CORE = (CZ, CY, CX)
FIELD = (EZ, EY, UX)
PART = (EZ * EY, CX)


def per_device(rhs_field, stiffness):
    *tables, inverse = solve_tables()
    strips = call(start_columns_kernel, [(16, 8, 128)] * 2, [rhs_field, stiffness])
    columns = swap(*strips, "gx")
    fields = [rhs_field, stiffness, *columns]
    strips = call(start_rows_kernel, [(START_Y, 8, 128)] * 2, fields[:2], cost=1.0)
    rows = swap(*strips, "gy")
    strips = call(start_corners_kernel, [(8, 8, 128)] * 2, columns, cost=5.0)
    corners = swap(*strips, "gy")
    wide, stiff, *strips = call(
        start_depth_kernel,
        [(CZ, EY, UX), (UZ, UY, UX)] + [(10, UY, CX)] * 2,
        [*fields, *rows, *corners],
    )
    depths = swap(*strips, "gz")
    fields = call(start_inner_kernel, [PART] * 2, [wide, *tables], cost=4.0)
    shape = Shape(False)
    solved, stiff, *strips = call(
        start_outer_kernel,
        [FIELD, (UZ, UY, UX)] + [(shape.x_tiles, 8, 128)] * 2,
        [*depths, stiff, *fields, inverse, *tables],
        [(4, EY, UX), PART, PART],
        cost=6.0,
    )
    smooth, image, sums = [], [], []
    for turn in range(ITERS):
        shape = Shape(turn + 1 == ITERS)
        columns = swap(*strips, "gx")
        strips = call(
            functools.partial(row_strips_kernel, shape),
            [(shape.y_tiles, 8, 128)] * 2,
            [solved],
            cost=1.0,
        )
        rows = swap(*strips, "gy")
        strips = call(
            functools.partial(corners_kernel, shape), [(shape.c_tiles, 8, 128)] * 2, columns, cost=5.0
        )
        corners = swap(*strips, "gy")
        widened = call(
            functools.partial(widen_kernel, shape), [(EZ, UY, UX)], [solved, *columns]
        )[0]
        folded, *strips = call(
            functools.partial(depth_strips_kernel, shape),
            [(EZ, UY, UX)] + [(shape.rim + 1, UY, CX)] * 2,
            [widened, *rows, *corners],
            [(4, 2 * shape.x_groups, 8, 128)],
        )
        depths = swap(*strips, "gz")
        products = (turn + 2, 8, 128)
        outs = [CORE, CORE, products]
        if not shape.last:
            outs += [PART, PART]
        own, core, part, *fields = call(
            functools.partial(inner_kernel, turn, shape),
            outs,
            [folded, stiff, rhs_field, *smooth] + ([] if shape.last else tables),
            ([] if shape.last else [FIELD]) + [(40, UY, UX)] * 2,
            cost=6.0,
        )
        operands = [folded, *depths, stiff, rhs_field, *smooth]
        operands += [own, core, part]
        scratch = [(14, UY, UX)] * 3
        if shape.last:
            operands += sums
            outs = [CORE, CORE, (8, 128)]
        else:
            operands += [*fields, inverse, *tables]
            following = Shape(turn + 2 == ITERS)
            outs = [CORE, CORE, products, FIELD] + [(following.x_tiles, 8, 128)] * 2
            scratch = [PART, PART, FIELD] + scratch
        own, core, part, *rest = call(
            functools.partial(outer_kernel, turn, shape),
            outs,
            operands,
            scratch,
            cost=8.0,
        )
        if rest:
            solved, *strips = rest
        smooth.append(own)
        image.append(core)
        sums.append(part)
    operands = [total(sums[-1]), rhs_field, *smooth, *image]
    return tuple(call(combine_kernel, [CORE] * 2, operands))


def solution(mesh):
    in_specs = (P("gz", "gy", "gx"), P("gz", "gy", "gx"))
    out_specs = (P("gz", "gy", "gx"), P("gz", "gy", "gx"))
    return jax.shard_map(
        per_device, mesh=mesh, in_specs=in_specs, out_specs=out_specs, check_vma=False
    )
```

profile of v0, /device:TPU:0, one launch (start us, length us, event | category | flops | bytes accessed | tf_op | source)
XLA Modules:
  0.0 167.0 jit_solution(2635212789439023345)
XLA Ops:
  0.6 1.1 copy-done
  1.8 1.1 copy-done.1
  2.9 0.9 shard_map.140
  3.8 4.0 %collective-permute-start = (f32[16,8,128]{2,1,0:T(8,128)S(1)}, f32[16,8,128]{2,1,0:T(8,128)S(1)}, u32[]{:S(2)}, u32[]{:S(2)}) collective-permute-start(f32[16,8,128]{2,1,0:T(8,128)S(1)} %get-tuple-element.67), channel_id=1, source_target_pairs={{0,16},{16,32},{32,48},{48,64},{64,80},{80,96},{96,112},{112,0},{1... | collective-permute-start | bytes 196616 | tf_op jit(solution)/shard_map/ppermute | solution.py:748
  7.8 2.3 %collective-permute-start.1 = (f32[16,8,128]{2,1,0:T(8,128)S(1)}, f32[16,8,128]{2,1,0:T(8,128)S(1)}, u32[]{:S(2)}, u32[]{:S(2)}) collective-permute-start(f32[16,8,128]{2,1,0:T(8,128)S(1)} %get-tuple-element.68), channel_id=1, source_target_pairs={{0,112},{16,0},{32,16},{48,32},{64,48},{80,64},{96,80},{112,96},{1... | collective-permute-start | bytes 196616 | tf_op jit(solution)/shard_map/ppermute | solution.py:748
  10.3 1.7 %collective-permute-start.3 = (f32[54,8,128]{2,1,0:T(8,128)S(1)}, f32[54,8,128]{2,1,0:T(8,128)S(1)}, u32[]{:S(2)}, u32[]{:S(2)}) collective-permute-start(f32[54,8,128]{2,1,0:T(8,128)S(1)} %get-tuple-element.70), channel_id=1, source_target_pairs={{0,12},{4,0},{8,4},{12,8},{1,13},{5,1},{9,5},{13,9},{2,14},{6,2},{... | collective-permute-start | bytes 663560 | tf_op jit(solution)/shard_map/ppermute | solution.py:748
  12.3 1.2 collective-permute-done.1.from_right
  13.7 1.8 %collective-permute-start.5 = (f32[8,8,128]{2,1,0:T(8,128)S(1)}, f32[8,8,128]{2,1,0:T(8,128)S(1)}, u32[]{:S(2)}, u32[]{:S(2)}) collective-permute-start(f32[8,8,128]{2,1,0:T(8,128)S(1)} %get-tuple-element.72), channel_id=1, source_target_pairs={{0,12},{4,0},{8,4},{12,8},{1,13},{5,1},{9,5},{13,9},{2,14},{6,2},{... | collective-permute-start | bytes 98312 | tf_op jit(solution)/shard_map/ppermute | solution.py:748
  15.4 1.9 %collective-permute-done.4.corner_near = f32[8,8,128]{2,1,0:T(8,128)S(1)} collective-permute-done((f32[8,8,128]{2,1,0:T(8,128)S(1)}, f32[8,8,128]{2,1,0:T(8,128)S(1)}, u32[]{:S(2)}, u32[]{:S(2)}) %collective-permute-start.4) | collective-permute-done | bytes 32800 | tf_op jit(solution)/shard_map/ppermute | solution.py:748
  17.6 1.5 shard_map.143
  19.1 1.6 collective-permute-start.6
  20.7 1.7 collective-permute-start.7
  22.4 3.0 %shard_map.144 = (f32[2240,128]{1,0:T(8,128)S(1)}, f32[2240,128]{1,0:T(8,128)S(1)}) custom-call(f32[48,40,256]{2,1,0:T(8,128)S(1)} %get-tuple-element.76.wide, bf16[256,256]{1,0:T(8,128)(2,1)S(1)} %copy-done.7, bf16[256,256]{1,0:T(8,128)(2,1)S(1)} %copy-done.6, bf16[256,256]{1,0:T(8,128)(2,1)S(1)} %copy-done.5, bf16[256,256]{1,0:T(8,128)(2,1)S(1)} %copy-done.4, ...), custom_call_target="tpu_custom_call" | custom-call | flops 4000000000 | bytes 14400000 | tf_op jit(solution)/shard_map/pallas_call | solution.py:733
  25.4 3.4 %collective-permute-done.6.from_below = f32[10,48,128]{2,1,0:T(8,128)S(1)} collective-permute-done((f32[10,48,128]{2,1,0:T(8,128)S(1)}, f32[10,48,128]{2,1,0:T(8,128)S(1)}, u32[]{:S(2)}, u32[]{:S(2)}) %collective-permute-start.6) | collective-permute-done | bytes 245792 | tf_op jit(solution)/shard_map/ppermute | solution.py:748
  29.5 5.0 %shard_map.145 = (f32[56,40,256]{2,1,0:T(8,128)S(1)}, f32[60,48,256]{2,1,0:T(8,128)S(1)}, f32[25,8,128]{2,1,0:T(8,128)S(1)}, f32[25,8,128]{2,1,0:T(8,128)S(1)}) custom-call(f32[10,48,128]{2,1,0:T(8,128)S(1)} %collective-permute-done.6.from_below, f32[10,48,128]{2,1,0:T(8,128)S(1)} %collective-permute-done.7.from_above, ...), custom_call_target="tpu_custom_call" | custom-call | flops 6000000000 | bytes 21600000 | tf_op jit(solution)/shard_map/pallas_call | solution.py:733
  34.5 1.8 %collective-permute-start.8 = (f32[25,8,128]{2,1,0:T(8,128)S(1)}, f32[25,8,128]{2,1,0:T(8,128)S(1)}, u32[]{:S(2)}, u32[]{:S(2)}) collective-permute-start(f32[25,8,128]{2,1,0:T(8,128)S(1)} %get-tuple-element.80), channel_id=1, source_target_pairs={{0,16},{16,32},{32,48},{48,64},{64,80},{80,96},{96,112},{112,0},{1... | collective-permute-start | bytes 307208 | tf_op jit(solution)/shard_map/ppermute | solution.py:748
  36.3 4.2 %collective-permute-start.9 = (f32[25,8,128]{2,1,0:T(8,128)S(1)}, f32[25,8,128]{2,1,0:T(8,128)S(1)}, u32[]{:S(2)}, u32[]{:S(2)}) collective-permute-start(f32[25,8,128]{2,1,0:T(8,128)S(1)} %get-tuple-element.81), channel_id=1, source_target_pairs={{0,112},{16,0},{32,16},{48,32},{64,48},{80,64},{96,80},{112,96},{1... | collective-permute-start | bytes 307208 | tf_op jit(solution)/shard_map/ppermute | solution.py:748
  40.9 1.7 %collective-permute-start.11 = (f32[75,8,128]{2,1,0:T(8,128)S(1)}, f32[75,8,128]{2,1,0:T(8,128)S(1)}, u32[]{:S(2)}, u32[]{:S(2)}) collective-permute-start(f32[75,8,128]{2,1,0:T(8,128)S(1)} %get-tuple-element.83), channel_id=1, source_target_pairs={{0,12},{4,0},{8,4},{12,8},{1,13},{5,1},{9,5},{13,9},{2,14},{6,2},{... | collective-permute-start | bytes 921608 | tf_op jit(solution)/shard_map/ppermute | solution.py:748
  43.2 2.2 %collective-permute-done.9.from_right = f32[25,8,128]{2,1,0:T(8,128)S(1)} collective-permute-done((f32[25,8,128]{2,1,0:T(8,128)S(1)}, f32[25,8,128]{2,1,0:T(8,128)S(1)}, u32[]{:S(2)}, u32[]{:S(2)}) %collective-permute-start.9) | collective-permute-done | bytes 102432 | tf_op jit(solution)/shard_map/ppermute | solution.py:748
  45.5 1.7 %collective-permute-start.13 = (f32[13,8,128]{2,1,0:T(8,128)S(1)}, f32[13,8,128]{2,1,0:T(8,128)S(1)}, u32[]{:S(2)}, u32[]{:S(2)}) collective-permute-start(f32[13,8,128]{2,1,0:T(8,128)S(1)} %get-tuple-element.85), channel_id=1, source_target_pairs={{0,12},{4,0},{8,4},{12,8},{1,13},{5,1},{9,5},{13,9},{2,14},{6,2},{... | collective-permute-start | bytes 159752 | tf_op jit(solution)/shard_map/ppermute | solution.py:748
  47.9 2.2 %collective-permute-done.12.corner_near = f32[13,8,128]{2,1,0:T(8,128)S(1)} collective-permute-done((f32[13,8,128]{2,1,0:T(8,128)S(1)}, f32[13,8,128]{2,1,0:T(8,128)S(1)}, u32[]{:S(2)}, u32[]{:S(2)}) %collective-permute-start.12) | collective-permute-done | bytes 53280 | tf_op jit(solution)/shard_map/ppermute | solution.py:748
  50.2 0.9 shard_map.149
  51.1 1.7 %collective-permute-start.14 = (f32[11,48,128]{2,1,0:T(8,128)S(1)}, f32[11,48,128]{2,1,0:T(8,128)S(1)}, u32[]{:S(2)}, u32[]{:S(2)}) collective-permute-start(f32[11,48,128]{2,1,0:T(8,128)S(1)} %get-tuple-element.87), channel_id=1, source_target_pairs={{0,1},{1,2},{2,3},{3,0},{4,5},{5,6},{6,7},{7,4},{8,9},{9,10},{10,1... | collective-permute-start | bytes 811016 | tf_op jit(solution)/shard_map/ppermute | solution.py:748
  52.8 1.6 collective-permute-start.15
  54.4 5.0 %shard_map.150 = (f32[48,32,128]{2,1,0:T(8,128)S(1)}, f32[48,32,128]{2,1,0:T(8,128)S(1)}, f32[2,8,128]{2,1,0:T(8,128)S(1)}, f32[2240,128]{1,0:T(8,128)S(1)}, f32[2240,128]{1,0:T(8,128)S(1)}) custom-call(f32[56,48,256]{2,1,0:T(8,128)S(1)} %get-tuple-element.86.refs_0_, f32[60,48,256]{2,1,0:T(8,128)S(1)} %get-tuple-element.89.refs_1_.refs_3_, ...), custom_call_target="tpu_custom_call" | custom-call | flops 6000000000 | bytes 21600000 | tf_op jit(solution)/shard_map/pallas_call | solution.py:733
  59.4 2.2 %collective-permute-done.14.refs_1_ = f32[11,48,128]{2,1,0:T(8,128)S(1)} collective-permute-done((f32[11,48,128]{2,1,0:T(8,128)S(1)}, f32[11,48,128]{2,1,0:T(8,128)S(1)}, u32[]{:S(2)}, u32[]{:S(2)}) %collective-permute-start.14) | collective-permute-done | bytes 270368 | tf_op jit(solution)/shard_map/ppermute | solution.py:748
  62.1 7.0 %shard_map.151 = (f32[48,32,128]{2,1,0:T(8,128)S(1)}, f32[48,32,128]{2,1,0:T(8,128)S(1)}, f32[2,8,128]{2,1,0:T(8,128)S(1)}, f32[56,40,256]{2,1,0:T(8,128)S(1)}, ...) custom-call(f32[56,48,256]{2,1,0:T(8,128)S(1)} %get-tuple-element.86.refs_0_, ...), custom_call_target="tpu_custom_call" | custom-call | flops 8000000000 | bytes 28800000 | tf_op jit(solution)/shard_map/pallas_call | solution.py:733
  69.1 13.6 %collective-permute-start.16 = (f32[25,8,128]{2,1,0:T(8,128)S(1)}, f32[25,8,128]{2,1,0:T(8,128)S(1)}, u32[]{:S(2)}, u32[]{:S(2)}) collective-permute-start(f32[25,8,128]{2,1,0:T(8,128)S(1)} %get-tuple-element.96), channel_id=1, source_target_pairs={{0,16},{16,32},{32,48},{48,64},{64,80},{80,96},{96,112},{112,0},{1... | collective-permute-start | bytes 307208 | tf_op jit(solution)/shard_map/ppermute | solution.py:748
  82.7 3.9 %collective-permute-start.17 = (f32[25,8,128]{2,1,0:T(8,128)S(1)}, f32[25,8,128]{2,1,0:T(8,128)S(1)}, u32[]{:S(2)}, u32[]{:S(2)}) collective-permute-start(f32[25,8,128]{2,1,0:T(8,128)S(1)} %get-tuple-element.97), channel_id=1, source_target_pairs={{0,112},{16,0},{32,16},{48,32},{64,48},{80,64},{96,80},{112,96},{1... | collective-permute-start | bytes 307208 | tf_op jit(solution)/shard_map/ppermute | solution.py:748
  86.9 1.7 %collective-permute-start.19 = (f32[75,8,128]{2,1,0:T(8,128)S(1)}, f32[75,8,128]{2,1,0:T(8,128)S(1)}, u32[]{:S(2)}, u32[]{:S(2)}) collective-permute-start(f32[75,8,128]{2,1,0:T(8,128)S(1)} %get-tuple-element.99), channel_id=1, source_target_pairs={{0,12},{4,0},{8,4},{12,8},{1,13},{5,1},{9,5},{13,9},{2,14},{6,2},{... | collective-permute-start | bytes 921608 | tf_op jit(solution)/shard_map/ppermute | solution.py:748
  88.7 0.8 collective-permute-done.16.from_left
  89.5 2.2 %collective-permute-done.17.from_right = f32[25,8,128]{2,1,0:T(8,128)S(1)} collective-permute-done((f32[25,8,128]{2,1,0:T(8,128)S(1)}, f32[25,8,128]{2,1,0:T(8,128)S(1)}, u32[]{:S(2)}, u32[]{:S(2)}) %collective-permute-start.17) | collective-permute-done | bytes 102432 | tf_op jit(solution)/shard_map/ppermute | solution.py:748
  91.8 1.7 %collective-permute-start.21 = (f32[13,8,128]{2,1,0:T(8,128)S(1)}, f32[13,8,128]{2,1,0:T(8,128)S(1)}, u32[]{:S(2)}, u32[]{:S(2)}) collective-permute-start(f32[13,8,128]{2,1,0:T(8,128)S(1)} %get-tuple-element.101), channel_id=1, source_target_pairs={{0,12},{4,0},{8,4},{12,8},{1,13},{5,1},{9,5},{13,9},{2,14},{6,2},{... | collective-permute-start | bytes 159752 | tf_op jit(solution)/shard_map/ppermute | solution.py:748
  94.2 1.9 %collective-permute-done.20.corner_near = f32[13,8,128]{2,1,0:T(8,128)S(1)} collective-permute-done((f32[13,8,128]{2,1,0:T(8,128)S(1)}, f32[13,8,128]{2,1,0:T(8,128)S(1)}, u32[]{:S(2)}, u32[]{:S(2)}) %collective-permute-start.20) | collective-permute-done | bytes 53280 | tf_op jit(solution)/shard_map/ppermute | solution.py:748
  96.3 0.9 shard_map.155
  97.2 1.3 collective-permute-start.22
  98.6 2.0 %collective-permute-start.23 = (f32[11,48,128]{2,1,0:T(8,128)S(1)}, f32[11,48,128]{2,1,0:T(8,128)S(1)}, u32[]{:S(2)}, u32[]{:S(2)}) collective-permute-start(f32[11,48,128]{2,1,0:T(8,128)S(1)} %get-tuple-element.104), channel_id=1, source_target_pairs={{0,3},{1,0},{2,1},{3,2},{4,7},{5,4},{6,5},{7,6},{8,11},{9,8},{10,9... | collective-permute-start | bytes 811016 | tf_op jit(solution)/shard_map/ppermute | solution.py:748
  100.5 5.0 %shard_map.156 = (f32[48,32,128]{2,1,0:T(8,128)S(1)}, f32[48,32,128]{2,1,0:T(8,128)S(1)}, f32[3,8,128]{2,1,0:T(8,128)S(1)}, f32[2240,128]{1,0:T(8,128)S(1)}, f32[2240,128]{1,0:T(8,128)S(1)}) custom-call(f32[56,48,256]{2,1,0:T(8,128)S(1)} %get-tuple-element.102.refs_0_, f32[60,48,256]{2,1,0:T(8,128)S(1)} %get-tuple-element.89.refs_1_.refs_3_, ...), custom_call_target="tpu_custom_call" | custom-call | flops 6000000000 | bytes 21600000 | tf_op jit(solution)/shard_map/pallas_call | solution.py:733
  105.5 2.1 %collective-permute-done.22.refs_1_ = f32[11,48,128]{2,1,0:T(8,128)S(1)} collective-permute-done((f32[11,48,128]{2,1,0:T(8,128)S(1)}, f32[11,48,128]{2,1,0:T(8,128)S(1)}, u32[]{:S(2)}, u32[]{:S(2)}) %collective-permute-start.22) | collective-permute-done | bytes 270368 | tf_op jit(solution)/shard_map/ppermute | solution.py:748
  107.9 7.0 %shard_map.157 = (f32[48,32,128]{2,1,0:T(8,128)S(1)}, f32[48,32,128]{2,1,0:T(8,128)S(1)}, f32[3,8,128]{2,1,0:T(8,128)S(1)}, f32[56,40,256]{2,1,0:T(8,128)S(1)}, ...) custom-call(f32[56,48,256]{2,1,0:T(8,128)S(1)} %get-tuple-element.102.refs_0_, ...), custom_call_target="tpu_custom_call" | custom-call | flops 8000000000 | bytes 28800000 | tf_op jit(solution)/shard_map/pallas_call | solution.py:733
  114.8 2.5 %collective-permute-start.24 = (f32[20,8,128]{2,1,0:T(8,128)S(1)}, f32[20,8,128]{2,1,0:T(8,128)S(1)}, u32[]{:S(2)}, u32[]{:S(2)}) collective-permute-start(f32[20,8,128]{2,1,0:T(8,128)S(1)} %get-tuple-element.112), channel_id=1, source_target_pairs={{0,16},{16,32},{32,48},{48,64},{64,80},{80,96},{96,112},{112,0},{1... | collective-permute-start | bytes 245768 | tf_op jit(solution)/shard_map/ppermute | solution.py:748
  117.3 3.2 %collective-permute-start.25 = (f32[20,8,128]{2,1,0:T(8,128)S(1)}, f32[20,8,128]{2,1,0:T(8,128)S(1)}, u32[]{:S(2)}, u32[]{:S(2)}) collective-permute-start(f32[20,8,128]{2,1,0:T(8,128)S(1)} %get-tuple-element.113), channel_id=1, source_target_pairs={{0,112},{16,0},{32,16},{48,32},{64,48},{80,64},{96,80},{112,96},{1... | collective-permute-start | bytes 245768 | tf_op jit(solution)/shard_map/ppermute | solution.py:748
  120.8 1.7 %collective-permute-start.27 = (f32[60,8,128]{2,1,0:T(8,128)S(1)}, f32[60,8,128]{2,1,0:T(8,128)S(1)}, u32[]{:S(2)}, u32[]{:S(2)}) collective-permute-start(f32[60,8,128]{2,1,0:T(8,128)S(1)} %get-tuple-element.115), channel_id=1, source_target_pairs={{0,12},{4,0},{8,4},{12,8},{1,13},{5,1},{9,5},{13,9},{2,14},{6,2},{... | collective-permute-start | bytes 737288 | tf_op jit(solution)/shard_map/ppermute | solution.py:748
  123.0 1.7 %collective-permute-done.25.from_right = f32[20,8,128]{2,1,0:T(8,128)S(1)} collective-permute-done((f32[20,8,128]{2,1,0:T(8,128)S(1)}, f32[20,8,128]{2,1,0:T(8,128)S(1)}, u32[]{:S(2)}, u32[]{:S(2)}) %collective-permute-start.25) | collective-permute-done | bytes 81952 | tf_op jit(solution)/shard_map/ppermute | solution.py:748
  124.8 1.7 %collective-permute-start.29 = (f32[8,8,128]{2,1,0:T(8,128)S(1)}, f32[8,8,128]{2,1,0:T(8,128)S(1)}, u32[]{:S(2)}, u32[]{:S(2)}) collective-permute-start(f32[8,8,128]{2,1,0:T(8,128)S(1)} %get-tuple-element.117), channel_id=1, source_target_pairs={{0,12},{4,0},{8,4},{12,8},{1,13},{5,1},{9,5},{13,9},{2,14},{6,2},{... | collective-permute-start | bytes 98312 | tf_op jit(solution)/shard_map/ppermute | solution.py:748
  127.2 1.3 collective-permute-done.28.corner_near
  128.6 0.7 shard_map.161
  129.3 1.5 collective-permute-start.30
  130.8 2.1 %collective-permute-start.31 = (f32[7,48,128]{2,1,0:T(8,128)S(1)}, f32[7,48,128]{2,1,0:T(8,128)S(1)}, u32[]{:S(2)}, u32[]{:S(2)}) collective-permute-start(f32[7,48,128]{2,1,0:T(8,128)S(1)} %get-tuple-element.120), channel_id=1, source_target_pairs={{0,3},{1,0},{2,1},{3,2},{4,7},{5,4},{6,5},{7,6},{8,11},{9,8},{10,9... | collective-permute-start | bytes 516104 | tf_op jit(solution)/shard_map/ppermute | solution.py:748
  132.9 2.2 %shard_map.162 = (f32[48,32,128]{2,1,0:T(8,128)S(1)}, f32[48,32,128]{2,1,0:T(8,128)S(1)}, f32[4,8,128]{2,1,0:T(8,128)S(1)}) custom-call(f32[56,48,256]{2,1,0:T(8,128)S(1)} %get-tuple-element.118.refs_0_, f32[60,48,256]{2,1,0:T(8,128)S(1)} %get-tuple-element.89.refs_1_.refs_3_, f32[48,32,128]{2,1,0:T(8,128)S(1)} %copy-done.2, ...), custom_call_target="tpu_custom_call" | custom-call | flops 6000000000 | bytes 21600000 | tf_op jit(solution)/shard_map/pallas_call | solution.py:733
  135.1 2.5 %collective-permute-done.30.refs_1_ = f32[7,48,128]{2,1,0:T(8,128)S(1)} collective-permute-done((f32[7,48,128]{2,1,0:T(8,128)S(1)}, f32[7,48,128]{2,1,0:T(8,128)S(1)}, u32[]{:S(2)}, u32[]{:S(2)}) %collective-permute-start.30) | collective-permute-done | bytes 172064 | tf_op jit(solution)/shard_map/ppermute | solution.py:748
  137.9 1.3 shard_map.163
  139.2 1.2 collective-permute-done.32
  140.4 1.6 collective-permute-start.35
  142.0 1.8 %collective-permute-start.34 = (f32[8,128]{1,0:T(8,128)S(1)}, f32[8,128]{1,0:T(8,128)S(1)}, u32[]{:S(2)}, u32[]{:S(2)}) collective-permute-start(f32[8,128]{1,0:T(8,128)S(1)} %add.30), channel_id=1, source_target_pairs={{0,16},{4,20},{8,24},{12,28},{16,0},{20,4},{24,8},{28,12},{32,48},... | collective-permute-start | bytes 12296 | tf_op jit(solution)/shard_map/ppermute | solution.py:762
  144.0 3.1 %collective-permute-done.34 = f32[8,128]{1,0:T(8,128)S(1)} collective-permute-done((f32[8,128]{1,0:T(8,128)S(1)}, f32[8,128]{1,0:T(8,128)S(1)}, u32[]{:S(2)}, u32[]{:S(2)}) %collective-permute-start.34) | collective-permute-done | bytes 4128 | tf_op jit(solution)/shard_map/ppermute | solution.py:762
  147.1 1.6 collective-permute-done.33
  148.7 2.8 %collective-permute-start.38 = (f32[8,128]{1,0:T(8,128)S(1)}, f32[8,128]{1,0:T(8,128)S(1)}, u32[]{:S(2)}, u32[]{:S(2)}) collective-permute-start(f32[8,128]{1,0:T(8,128)S(1)} %add_add_fusion.2), channel_id=1, source_target_pairs={{0,96},{16,112},{32,0},{48,16},{64,32},{80,48},{96,64},{112,80},{1... | collective-permute-start | bytes 12296 | tf_op jit(solution)/shard_map/ppermute | solution.py:762
  151.5 0.9 collective-permute-start.36
  152.8 3.8 %collective-permute-done.37 = f32[8,128]{1,0:T(8,128)S(1)} collective-permute-done((f32[8,128]{1,0:T(8,128)S(1)}, f32[8,128]{1,0:T(8,128)S(1)}, u32[]{:S(2)}, u32[]{:S(2)}) %collective-permute-start.37) | collective-permute-done | bytes 4128 | tf_op jit(solution)/shard_map/ppermute | solution.py:762
  156.6 3.3 %collective-permute-start.41 = (f32[8,128]{1,0:T(8,128)S(1)}, f32[8,128]{1,0:T(8,128)S(1)}, u32[]{:S(2)}, u32[]{:S(2)}) collective-permute-start(f32[8,128]{1,0:T(8,128)S(1)} %add_add_fusion.1), channel_id=1, source_target_pairs={{0,3},{1,0},{2,1},{3,2},{4,7},{5,4},{6,5},{7,6},{8,11},{9,8},{10,9... | collective-permute-start | bytes 12296 | tf_op jit(solution)/shard_map/ppermute | solution.py:762
  160.2 1.0 collective-permute-start.39
  161.2 3.8 %collective-permute-done.40 = f32[8,128]{1,0:T(8,128)S(1)} collective-permute-done((f32[8,128]{1,0:T(8,128)S(1)}, f32[8,128]{1,0:T(8,128)S(1)}, u32[]{:S(2)}, u32[]{:S(2)}) %collective-permute-start.40) | collective-permute-done | bytes 4128 | tf_op jit(solution)/shard_map/ppermute | solution.py:762
  165.0 1.7 %shard_map.164 = (f32[48,32,128]{2,1,0:T(8,128)}, f32[48,32,128]{2,1,0:T(8,128)}) custom-call(f32[8,128]{1,0:T(8,128)S(1)} %add_add_fusion.sums, f32[48,32,128]{2,1,0:T(8,128)S(1)} %copy-done.2, f32[48,32,128]{2,1,0:T(8,128)S(1)} %get-tuple-element.105.refs_3_.refs_5_.u0, f32[48,32,128]{2,1,0:T(8,128)S(1)} %get-tuple-element.121.refs_4_.refs_6_.u1, ...), custom_call_target="tpu_custom_call" | custom-call | flops 2000000000 | bytes 7200000 | tf_op jit(solution)/shard_map/pallas_call | solution.py:733
  (71 shorter events, 8.1 us)
Async XLA Ops:
  0.6 1.1 copy-start
  1.8 1.1 copy-start.1
  3.8 8.6 %collective-permute-start = (f32[16,8,128]{2,1,0:T(8,128)S(1)}, f32[16,8,128]{2,1,0:T(8,128)S(1)}, u32[]{:S(2)}, u32[]{:S(2)}) collective-permute-start(f32[16,8,128]{2,1,0:T(8,128)S(1)} %get-tuple-element.67), channel_id=1, source_target_pairs={{0,16},{16,32},{32,48},{48,64},{64,80},{80,96},{96,112},{112,0},{1... | collective-permute-start | bytes 196616 | tf_op jit(solution)/shard_map/ppermute | solution.py:748
  7.8 5.8 %collective-permute-start.1 = (f32[16,8,128]{2,1,0:T(8,128)S(1)}, f32[16,8,128]{2,1,0:T(8,128)S(1)}, u32[]{:S(2)}, u32[]{:S(2)}) collective-permute-start(f32[16,8,128]{2,1,0:T(8,128)S(1)} %get-tuple-element.68), channel_id=1, source_target_pairs={{0,112},{16,0},{32,16},{48,32},{64,48},{80,64},{96,80},{112,96},{1... | collective-permute-start | bytes 196616 | tf_op jit(solution)/shard_map/ppermute | solution.py:748
  10.2 7.4 %collective-permute-start.2 = (f32[54,8,128]{2,1,0:T(8,128)S(1)}, f32[54,8,128]{2,1,0:T(8,128)S(1)}, u32[]{:S(2)}, u32[]{:S(2)}) collective-permute-start(f32[54,8,128]{2,1,0:T(8,128)S(1)} %get-tuple-element.69), channel_id=1, source_target_pairs={{0,4},{4,8},{8,12},{12,0},{1,5},{5,9},{9,13},{13,1},{2,6},{6,10},{... | collective-permute-start | bytes 663560 | tf_op jit(solution)/shard_map/ppermute | solution.py:748
  10.3 7.3 %copy-start.2 = (f32[48,32,128]{2,1,0:T(8,128)S(1)}, f32[48,32,128]{2,1,0:T(8,128)}, u32[]{:S(2)}) copy-start(f32[48,32,128]{2,1,0:T(8,128)} %rhs.7) | copy-start | bytes 2359300
  10.3 7.3 %collective-permute-start.3 = (f32[54,8,128]{2,1,0:T(8,128)S(1)}, f32[54,8,128]{2,1,0:T(8,128)S(1)}, u32[]{:S(2)}, u32[]{:S(2)}) collective-permute-start(f32[54,8,128]{2,1,0:T(8,128)S(1)} %get-tuple-element.70), channel_id=1, source_target_pairs={{0,12},{4,0},{8,4},{12,8},{1,13},{5,1},{9,5},{13,9},{2,14},{6,2},{... | collective-permute-start | bytes 663560 | tf_op jit(solution)/shard_map/ppermute | solution.py:748
  13.6 3.7 %collective-permute-start.4 = (f32[8,8,128]{2,1,0:T(8,128)S(1)}, f32[8,8,128]{2,1,0:T(8,128)S(1)}, u32[]{:S(2)}, u32[]{:S(2)}) collective-permute-start(f32[8,8,128]{2,1,0:T(8,128)S(1)} %get-tuple-element.71), channel_id=1, source_target_pairs={{0,4},{4,8},{8,12},{12,0},{1,5},{5,9},{9,13},{13,1},{2,6},{6,10},{... | collective-permute-start | bytes 98312 | tf_op jit(solution)/shard_map/ppermute | solution.py:748
  13.6 8.8 %copy-start.4 = (bf16[256,256]{1,0:T(8,128)(2,1)S(1)}, bf16[256,256]{1,0:T(8,128)(2,1)}, u32[]{:S(2)}) copy-start(bf16[256,256]{1,0:T(8,128)(2,1)} %constant.25.clone.refs_3_.refs_6_.refs_14_.refs_7_.refs_15_) | copy-start | bytes 393220
  13.6 8.8 %copy-start.5 = (bf16[256,256]{1,0:T(8,128)(2,1)S(1)}, bf16[256,256]{1,0:T(8,128)(2,1)}, u32[]{:S(2)}) copy-start(bf16[256,256]{1,0:T(8,128)(2,1)} %constant.24.clone.refs_2_.refs_5_.refs_13_.refs_6_.refs_14_) | copy-start | bytes 393220
  13.6 8.8 %copy-start.6 = (bf16[256,256]{1,0:T(8,128)(2,1)S(1)}, bf16[256,256]{1,0:T(8,128)(2,1)}, u32[]{:S(2)}) copy-start(bf16[256,256]{1,0:T(8,128)(2,1)} %constant.23.clone.refs_1_.refs_4_.refs_12_.refs_5_.refs_13_) | copy-start | bytes 393220
  13.6 8.8 %copy-start.7 = (bf16[256,256]{1,0:T(8,128)(2,1)S(1)}, bf16[256,256]{1,0:T(8,128)(2,1)}, u32[]{:S(2)}) copy-start(bf16[256,256]{1,0:T(8,128)(2,1)} %constant.22.clone.refs_0_.refs_3_.refs_11_.refs_4_.refs_12_) | copy-start | bytes 393220
  13.6 8.8 %copy-start.8 = (bf16[80,240]{1,0:T(8,128)(2,1)S(1)}, bf16[80,240]{1,0:T(8,128)(2,1)}, u32[]{:S(2)}) copy-start(bf16[80,240]{1,0:T(8,128)(2,1)} %constant.34.refs_5_.refs_8_.refs_16_.refs_9_.refs_17_) | copy-start | bytes 115204
  13.6 8.8 %copy-start.9 = (bf16[80,240]{1,0:T(8,128)(2,1)S(1)}, bf16[80,240]{1,0:T(8,128)(2,1)}, u32[]{:S(2)}) copy-start(bf16[80,240]{1,0:T(8,128)(2,1)} %constant.33.refs_4_.refs_7_.refs_15_.refs_8_.refs_16_) | copy-start | bytes 115204
  13.6 8.8 %copy-start.10 = (bf16[56,168]{1,0:T(8,128)(2,1)S(1)}, bf16[56,168]{1,0:T(8,128)(2,1)}, u32[]{:S(2)}) copy-start(bf16[56,168]{1,0:T(8,128)(2,1)} %constant.35.refs_6_.refs_9_.refs_17_.refs_10_.refs_18_) | copy-start | bytes 56452
  13.7 3.9 %collective-permute-start.5 = (f32[8,8,128]{2,1,0:T(8,128)S(1)}, f32[8,8,128]{2,1,0:T(8,128)S(1)}, u32[]{:S(2)}, u32[]{:S(2)}) collective-permute-start(f32[8,8,128]{2,1,0:T(8,128)S(1)} %get-tuple-element.72), channel_id=1, source_target_pairs={{0,12},{4,0},{8,4},{12,8},{1,13},{5,1},{9,5},{13,9},{2,14},{6,2},{... | collective-permute-start | bytes 98312 | tf_op jit(solution)/shard_map/ppermute | solution.py:748
  19.1 9.8 %collective-permute-start.6 = (f32[10,48,128]{2,1,0:T(8,128)S(1)}, f32[10,48,128]{2,1,0:T(8,128)S(1)}, u32[]{:S(2)}, u32[]{:S(2)}) collective-permute-start(f32[10,48,128]{2,1,0:T(8,128)S(1)} %get-tuple-element.73), channel_id=1, source_target_pairs={{0,1},{1,2},{2,3},{3,0},{4,5},{5,6},{6,7},{7,4},{8,9},{9,10},{10,1... | collective-permute-start | bytes 737288 | tf_op jit(solution)/shard_map/ppermute | solution.py:748
  20.7 8.8 %collective-permute-start.7 = (f32[10,48,128]{2,1,0:T(8,128)S(1)}, f32[10,48,128]{2,1,0:T(8,128)S(1)}, u32[]{:S(2)}, u32[]{:S(2)}) collective-permute-start(f32[10,48,128]{2,1,0:T(8,128)S(1)} %get-tuple-element.74), channel_id=1, source_target_pairs={{0,3},{1,0},{2,1},{3,2},{4,7},{5,4},{6,5},{7,6},{8,11},{9,8},{10,9... | collective-permute-start | bytes 737288 | tf_op jit(solution)/shard_map/ppermute | solution.py:748
  22.4 7.1 %copy-start.3 = (f32[40,56,256]{2,1,0:T(8,128)S(1)}, f32[40,56,256]{2,1,0:T(8,128)}, u32[]{:S(2)}) copy-start(f32[40,56,256]{2,1,0:T(8,128)} %constant.32.clone.refs_2_.refs_10_.refs_11_) | copy-start | bytes 6881284
  34.5 8.7 %collective-permute-start.8 = (f32[25,8,128]{2,1,0:T(8,128)S(1)}, f32[25,8,128]{2,1,0:T(8,128)S(1)}, u32[]{:S(2)}, u32[]{:S(2)}) collective-permute-start(f32[25,8,128]{2,1,0:T(8,128)S(1)} %get-tuple-element.80), channel_id=1, source_target_pairs={{0,16},{16,32},{32,48},{48,64},{64,80},{80,96},{96,112},{112,0},{1... | collective-permute-start | bytes 307208 | tf_op jit(solution)/shard_map/ppermute | solution.py:748
  36.3 9.1 %collective-permute-start.9 = (f32[25,8,128]{2,1,0:T(8,128)S(1)}, f32[25,8,128]{2,1,0:T(8,128)S(1)}, u32[]{:S(2)}, u32[]{:S(2)}) collective-permute-start(f32[25,8,128]{2,1,0:T(8,128)S(1)} %get-tuple-element.81), channel_id=1, source_target_pairs={{0,112},{16,0},{32,16},{48,32},{64,48},{80,64},{96,80},{112,96},{1... | collective-permute-start | bytes 307208 | tf_op jit(solution)/shard_map/ppermute | solution.py:748
  40.8 9.4 %collective-permute-start.10 = (f32[75,8,128]{2,1,0:T(8,128)S(1)}, f32[75,8,128]{2,1,0:T(8,128)S(1)}, u32[]{:S(2)}, u32[]{:S(2)}) collective-permute-start(f32[75,8,128]{2,1,0:T(8,128)S(1)} %get-tuple-element.82), channel_id=1, source_target_pairs={{0,4},{4,8},{8,12},{12,0},{1,5},{5,9},{9,13},{13,1},{2,6},{6,10},{... | collective-permute-start | bytes 921608 | tf_op jit(solution)/shard_map/ppermute | solution.py:748
  40.9 9.3 %collective-permute-start.11 = (f32[75,8,128]{2,1,0:T(8,128)S(1)}, f32[75,8,128]{2,1,0:T(8,128)S(1)}, u32[]{:S(2)}, u32[]{:S(2)}) collective-permute-start(f32[75,8,128]{2,1,0:T(8,128)S(1)} %get-tuple-element.83), channel_id=1, source_target_pairs={{0,12},{4,0},{8,4},{12,8},{1,13},{5,1},{9,5},{13,9},{2,14},{6,2},{... | collective-permute-start | bytes 921608 | tf_op jit(solution)/shard_map/ppermute | solution.py:748
  45.4 4.7 %collective-permute-start.12 = (f32[13,8,128]{2,1,0:T(8,128)S(1)}, f32[13,8,128]{2,1,0:T(8,128)S(1)}, u32[]{:S(2)}, u32[]{:S(2)}) collective-permute-start(f32[13,8,128]{2,1,0:T(8,128)S(1)} %get-tuple-element.84), channel_id=1, source_target_pairs={{0,4},{4,8},{8,12},{12,0},{1,5},{5,9},{9,13},{13,1},{2,6},{6,10},{... | collective-permute-start | bytes 159752 | tf_op jit(solution)/shard_map/ppermute | solution.py:748
  45.5 4.7 %collective-permute-start.13 = (f32[13,8,128]{2,1,0:T(8,128)S(1)}, f32[13,8,128]{2,1,0:T(8,128)S(1)}, u32[]{:S(2)}, u32[]{:S(2)}) collective-permute-start(f32[13,8,128]{2,1,0:T(8,128)S(1)} %get-tuple-element.85), channel_id=1, source_target_pairs={{0,12},{4,0},{8,4},{12,8},{1,13},{5,1},{9,5},{13,9},{2,14},{6,2},{... | collective-permute-start | bytes 159752 | tf_op jit(solution)/shard_map/ppermute | solution.py:748
  51.1 10.4 %collective-permute-start.14 = (f32[11,48,128]{2,1,0:T(8,128)S(1)}, f32[11,48,128]{2,1,0:T(8,128)S(1)}, u32[]{:S(2)}, u32[]{:S(2)}) collective-permute-start(f32[11,48,128]{2,1,0:T(8,128)S(1)} %get-tuple-element.87), channel_id=1, source_target_pairs={{0,1},{1,2},{2,3},{3,0},{4,5},{5,6},{6,7},{7,4},{8,9},{9,10},{10,1... | collective-permute-start | bytes 811016 | tf_op jit(solution)/shard_map/ppermute | solution.py:748
  52.8 9.3 %collective-permute-start.15 = (f32[11,48,128]{2,1,0:T(8,128)S(1)}, f32[11,48,128]{2,1,0:T(8,128)S(1)}, u32[]{:S(2)}, u32[]{:S(2)}) collective-permute-start(f32[11,48,128]{2,1,0:T(8,128)S(1)} %get-tuple-element.88), channel_id=1, source_target_pairs={{0,3},{1,0},{2,1},{3,2},{4,7},{5,4},{6,5},{7,6},{8,11},{9,8},{10,9... | collective-permute-start | bytes 811016 | tf_op jit(solution)/shard_map/ppermute | solution.py:748
  69.1 20.4 %collective-permute-start.16 = (f32[25,8,128]{2,1,0:T(8,128)S(1)}, f32[25,8,128]{2,1,0:T(8,128)S(1)}, u32[]{:S(2)}, u32[]{:S(2)}) collective-permute-start(f32[25,8,128]{2,1,0:T(8,128)S(1)} %get-tuple-element.96), channel_id=1, source_target_pairs={{0,16},{16,32},{32,48},{48,64},{64,80},{80,96},{96,112},{112,0},{1... | collective-permute-start | bytes 307208 | tf_op jit(solution)/shard_map/ppermute | solution.py:748
  82.7 9.0 %collective-permute-start.17 = (f32[25,8,128]{2,1,0:T(8,128)S(1)}, f32[25,8,128]{2,1,0:T(8,128)S(1)}, u32[]{:S(2)}, u32[]{:S(2)}) collective-permute-start(f32[25,8,128]{2,1,0:T(8,128)S(1)} %get-tuple-element.97), channel_id=1, source_target_pairs={{0,112},{16,0},{32,16},{48,32},{64,48},{80,64},{96,80},{112,96},{1... | collective-permute-start | bytes 307208 | tf_op jit(solution)/shard_map/ppermute | solution.py:748
  86.8 9.5 %collective-permute-start.18 = (f32[75,8,128]{2,1,0:T(8,128)S(1)}, f32[75,8,128]{2,1,0:T(8,128)S(1)}, u32[]{:S(2)}, u32[]{:S(2)}) collective-permute-start(f32[75,8,128]{2,1,0:T(8,128)S(1)} %get-tuple-element.98), channel_id=1, source_target_pairs={{0,4},{4,8},{8,12},{12,0},{1,5},{5,9},{9,13},{13,1},{2,6},{6,10},{... | collective-permute-start | bytes 921608 | tf_op jit(solution)/shard_map/ppermute | solution.py:748
  86.9 9.4 %collective-permute-start.19 = (f32[75,8,128]{2,1,0:T(8,128)S(1)}, f32[75,8,128]{2,1,0:T(8,128)S(1)}, u32[]{:S(2)}, u32[]{:S(2)}) collective-permute-start(f32[75,8,128]{2,1,0:T(8,128)S(1)} %get-tuple-element.99), channel_id=1, source_target_pairs={{0,12},{4,0},{8,4},{12,8},{1,13},{5,1},{9,5},{13,9},{2,14},{6,2},{... | collective-permute-start | bytes 921608 | tf_op jit(solution)/shard_map/ppermute | solution.py:748
  91.7 4.4 %collective-permute-start.20 = (f32[13,8,128]{2,1,0:T(8,128)S(1)}, f32[13,8,128]{2,1,0:T(8,128)S(1)}, u32[]{:S(2)}, u32[]{:S(2)}) collective-permute-start(f32[13,8,128]{2,1,0:T(8,128)S(1)} %get-tuple-element.100), channel_id=1, source_target_pairs={{0,4},{4,8},{8,12},{12,0},{1,5},{5,9},{9,13},{13,1},{2,6},{6,10},{... | collective-permute-start | bytes 159752 | tf_op jit(solution)/shard_map/ppermute | solution.py:748
  91.8 4.5 %collective-permute-start.21 = (f32[13,8,128]{2,1,0:T(8,128)S(1)}, f32[13,8,128]{2,1,0:T(8,128)S(1)}, u32[]{:S(2)}, u32[]{:S(2)}) collective-permute-start(f32[13,8,128]{2,1,0:T(8,128)S(1)} %get-tuple-element.101), channel_id=1, source_target_pairs={{0,12},{4,0},{8,4},{12,8},{1,13},{5,1},{9,5},{13,9},{2,14},{6,2},{... | collective-permute-start | bytes 159752 | tf_op jit(solution)/shard_map/ppermute | solution.py:748
  97.2 10.4 %collective-permute-start.22 = (f32[11,48,128]{2,1,0:T(8,128)S(1)}, f32[11,48,128]{2,1,0:T(8,128)S(1)}, u32[]{:S(2)}, u32[]{:S(2)}) collective-permute-start(f32[11,48,128]{2,1,0:T(8,128)S(1)} %get-tuple-element.103), channel_id=1, source_target_pairs={{0,1},{1,2},{2,3},{3,0},{4,5},{5,6},{6,7},{7,4},{8,9},{9,10},{10,1... | collective-permute-start | bytes 811016 | tf_op jit(solution)/shard_map/ppermute | solution.py:748
  98.6 9.3 %collective-permute-start.23 = (f32[11,48,128]{2,1,0:T(8,128)S(1)}, f32[11,48,128]{2,1,0:T(8,128)S(1)}, u32[]{:S(2)}, u32[]{:S(2)}) collective-permute-start(f32[11,48,128]{2,1,0:T(8,128)S(1)} %get-tuple-element.104), channel_id=1, source_target_pairs={{0,3},{1,0},{2,1},{3,2},{4,7},{5,4},{6,5},{7,6},{8,11},{9,8},{10,9... | collective-permute-start | bytes 811016 | tf_op jit(solution)/shard_map/ppermute | solution.py:748
  114.8 8.1 %collective-permute-start.24 = (f32[20,8,128]{2,1,0:T(8,128)S(1)}, f32[20,8,128]{2,1,0:T(8,128)S(1)}, u32[]{:S(2)}, u32[]{:S(2)}) collective-permute-start(f32[20,8,128]{2,1,0:T(8,128)S(1)} %get-tuple-element.112), channel_id=1, source_target_pairs={{0,16},{16,32},{32,48},{48,64},{64,80},{80,96},{96,112},{112,0},{1... | collective-permute-start | bytes 245768 | tf_op jit(solution)/shard_map/ppermute | solution.py:748
  117.3 7.4 %collective-permute-start.25 = (f32[20,8,128]{2,1,0:T(8,128)S(1)}, f32[20,8,128]{2,1,0:T(8,128)S(1)}, u32[]{:S(2)}, u32[]{:S(2)}) collective-permute-start(f32[20,8,128]{2,1,0:T(8,128)S(1)} %get-tuple-element.113), channel_id=1, source_target_pairs={{0,112},{16,0},{32,16},{48,32},{64,48},{80,64},{96,80},{112,96},{1... | collective-permute-start | bytes 245768 | tf_op jit(solution)/shard_map/ppermute | solution.py:748
  120.8 7.8 %collective-permute-start.26 = (f32[60,8,128]{2,1,0:T(8,128)S(1)}, f32[60,8,128]{2,1,0:T(8,128)S(1)}, u32[]{:S(2)}, u32[]{:S(2)}) collective-permute-start(f32[60,8,128]{2,1,0:T(8,128)S(1)} %get-tuple-element.114), channel_id=1, source_target_pairs={{0,4},{4,8},{8,12},{12,0},{1,5},{5,9},{9,13},{13,1},{2,6},{6,10},{... | collective-permute-start | bytes 737288 | tf_op jit(solution)/shard_map/ppermute | solution.py:748
  120.8 7.7 %collective-permute-start.27 = (f32[60,8,128]{2,1,0:T(8,128)S(1)}, f32[60,8,128]{2,1,0:T(8,128)S(1)}, u32[]{:S(2)}, u32[]{:S(2)}) collective-permute-start(f32[60,8,128]{2,1,0:T(8,128)S(1)} %get-tuple-element.115), channel_id=1, source_target_pairs={{0,12},{4,0},{8,4},{12,8},{1,13},{5,1},{9,5},{13,9},{2,14},{6,2},{... | collective-permute-start | bytes 737288 | tf_op jit(solution)/shard_map/ppermute | solution.py:748
  124.7 3.8 %collective-permute-start.28 = (f32[8,8,128]{2,1,0:T(8,128)S(1)}, f32[8,8,128]{2,1,0:T(8,128)S(1)}, u32[]{:S(2)}, u32[]{:S(2)}) collective-permute-start(f32[8,8,128]{2,1,0:T(8,128)S(1)} %get-tuple-element.116), channel_id=1, source_target_pairs={{0,4},{4,8},{8,12},{12,0},{1,5},{5,9},{9,13},{13,1},{2,6},{6,10},{... | collective-permute-start | bytes 98312 | tf_op jit(solution)/shard_map/ppermute | solution.py:748
  124.8 3.7 %collective-permute-start.29 = (f32[8,8,128]{2,1,0:T(8,128)S(1)}, f32[8,8,128]{2,1,0:T(8,128)S(1)}, u32[]{:S(2)}, u32[]{:S(2)}) collective-permute-start(f32[8,8,128]{2,1,0:T(8,128)S(1)} %get-tuple-element.117), channel_id=1, source_target_pairs={{0,12},{4,0},{8,4},{12,8},{1,13},{5,1},{9,5},{13,9},{2,14},{6,2},{... | collective-permute-start | bytes 98312 | tf_op jit(solution)/shard_map/ppermute | solution.py:748
  129.3 8.3 %collective-permute-start.30 = (f32[7,48,128]{2,1,0:T(8,128)S(1)}, f32[7,48,128]{2,1,0:T(8,128)S(1)}, u32[]{:S(2)}, u32[]{:S(2)}) collective-permute-start(f32[7,48,128]{2,1,0:T(8,128)S(1)} %get-tuple-element.119), channel_id=1, source_target_pairs={{0,1},{1,2},{2,3},{3,0},{4,5},{5,6},{6,7},{7,4},{8,9},{9,10},{10,1... | collective-permute-start | bytes 516104 | tf_op jit(solution)/shard_map/ppermute | solution.py:748
  130.8 7.1 %collective-permute-start.31 = (f32[7,48,128]{2,1,0:T(8,128)S(1)}, f32[7,48,128]{2,1,0:T(8,128)S(1)}, u32[]{:S(2)}, u32[]{:S(2)}) collective-permute-start(f32[7,48,128]{2,1,0:T(8,128)S(1)} %get-tuple-element.120), channel_id=1, source_target_pairs={{0,3},{1,0},{2,1},{3,2},{4,7},{5,4},{6,5},{7,6},{8,11},{9,8},{10,9... | collective-permute-start | bytes 516104 | tf_op jit(solution)/shard_map/ppermute | solution.py:748
  139.2 1.2 collective-permute-start.32
  140.4 3.6 %collective-permute-start.35 = (f32[8,128]{1,0:T(8,128)S(1)}, f32[8,128]{1,0:T(8,128)S(1)}, u32[]{:S(2)}, u32[]{:S(2)}) collective-permute-start(f32[8,128]{1,0:T(8,128)S(1)} %add.30), channel_id=1, source_target_pairs={{0,24},{4,28},{8,0},{12,4},{16,8},{20,12},{24,16},{28,20},{32,56},... | collective-permute-start | bytes 12296 | tf_op jit(solution)/shard_map/ppermute | solution.py:762
  142.0 5.1 %collective-permute-start.34 = (f32[8,128]{1,0:T(8,128)S(1)}, f32[8,128]{1,0:T(8,128)S(1)}, u32[]{:S(2)}, u32[]{:S(2)}) collective-permute-start(f32[8,128]{1,0:T(8,128)S(1)} %add.30), channel_id=1, source_target_pairs={{0,16},{4,20},{8,24},{12,28},{16,0},{20,4},{24,8},{28,12},{32,48},... | collective-permute-start | bytes 12296 | tf_op jit(solution)/shard_map/ppermute | solution.py:762
  143.9 4.8 %collective-permute-start.33 = (f32[8,128]{1,0:T(8,128)S(1)}, f32[8,128]{1,0:T(8,128)S(1)}, u32[]{:S(2)}, u32[]{:S(2)}) collective-permute-start(f32[8,128]{1,0:T(8,128)S(1)} %add.30), channel_id=1, source_target_pairs={{0,8},{4,12},{8,16},{12,20},{16,24},{20,28},{24,0},{28,4},{32,40},... | collective-permute-start | bytes 12296 | tf_op jit(solution)/shard_map/ppermute | solution.py:762
  148.7 4.1 %collective-permute-start.38 = (f32[8,128]{1,0:T(8,128)S(1)}, f32[8,128]{1,0:T(8,128)S(1)}, u32[]{:S(2)}, u32[]{:S(2)}) collective-permute-start(f32[8,128]{1,0:T(8,128)S(1)} %add_add_fusion.2), channel_id=1, source_target_pairs={{0,96},{16,112},{32,0},{48,16},{64,32},{80,48},{96,64},{112,80},{1... | collective-permute-start | bytes 12296 | tf_op jit(solution)/shard_map/ppermute | solution.py:762
  151.4 5.1 %collective-permute-start.37 = (f32[8,128]{1,0:T(8,128)S(1)}, f32[8,128]{1,0:T(8,128)S(1)}, u32[]{:S(2)}, u32[]{:S(2)}) collective-permute-start(f32[8,128]{1,0:T(8,128)S(1)} %add_add_fusion.2), channel_id=1, source_target_pairs={{0,64},{16,80},{32,96},{48,112},{64,0},{80,16},{96,32},{112,48},{1... | collective-permute-start | bytes 12296 | tf_op jit(solution)/shard_map/ppermute | solution.py:762
  151.5 5.1 %collective-permute-start.36 = (f32[8,128]{1,0:T(8,128)S(1)}, f32[8,128]{1,0:T(8,128)S(1)}, u32[]{:S(2)}, u32[]{:S(2)}) collective-permute-start(f32[8,128]{1,0:T(8,128)S(1)} %add_add_fusion.2), channel_id=1, source_target_pairs={{0,32},{16,48},{32,64},{48,80},{64,96},{80,112},{96,0},{112,16},{1... | collective-permute-start | bytes 12296 | tf_op jit(solution)/shard_map/ppermute | solution.py:762
  156.6 4.6 %collective-permute-start.41 = (f32[8,128]{1,0:T(8,128)S(1)}, f32[8,128]{1,0:T(8,128)S(1)}, u32[]{:S(2)}, u32[]{:S(2)}) collective-permute-start(f32[8,128]{1,0:T(8,128)S(1)} %add_add_fusion.1), channel_id=1, source_target_pairs={{0,3},{1,0},{2,1},{3,2},{4,7},{5,4},{6,5},{7,6},{8,11},{9,8},{10,9... | collective-permute-start | bytes 12296 | tf_op jit(solution)/shard_map/ppermute | solution.py:762
  159.9 5.1 %collective-permute-start.40 = (f32[8,128]{1,0:T(8,128)S(1)}, f32[8,128]{1,0:T(8,128)S(1)}, u32[]{:S(2)}, u32[]{:S(2)}) collective-permute-start(f32[8,128]{1,0:T(8,128)S(1)} %add_add_fusion.1), channel_id=1, source_target_pairs={{0,2},{1,3},{2,0},{3,1},{4,6},{5,7},{6,4},{7,5},{8,10},{9,11},{10,... | collective-permute-start | bytes 12296 | tf_op jit(solution)/shard_map/ppermute | solution.py:762
  160.2 4.8 %collective-permute-start.39 = (f32[8,128]{1,0:T(8,128)S(1)}, f32[8,128]{1,0:T(8,128)S(1)}, u32[]{:S(2)}, u32[]{:S(2)}) collective-permute-start(f32[8,128]{1,0:T(8,128)S(1)} %add_add_fusion.1), channel_id=1, source_target_pairs={{0,1},{1,2},{2,3},{3,0},{4,5},{5,6},{6,7},{7,4},{8,9},{9,10},{10,1... | collective-permute-start | bytes 12296 | tf_op jit(solution)/shard_map/ppermute | solution.py:762
where the time goes:
time: 170 us; the launch traced here: 167 us
  starting transfers between devices  75.2 us (44%)
  Pallas kernels  44.9 us (26%)
  waiting for transfers between devices  43.3 us (25%)
  local copies, waits for them, and re-layouts  2.32 us (1%)
    ppermute x32, starting transfers between devices, shifted(): lax.ppermute(block, axis, [(i, (i + step) % count) for i in range(count)])  63.4 us
    pallas_call x25, Pallas kernels, call(): pl.pallas_call(kernel, out_shape=[jax.ShapeDtypeStruct(shape, f32) for sh...  44.9 us
    ppermute x32, waiting for transfers between devices, shifted(): lax.ppermute(block, axis, [(i, (i + step) % count) for i in range(count)])  29.3 us
    ppermute x10, waiting for transfers between devices, ring(): parts.append(lax.ppermute(values, axes, route))  14 us
    ppermute x10, starting transfers between devices, ring(): parts.append(lax.ppermute(values, axes, route))  11.8 us
  transfers between devices with their start and end apart: 42, of which 30 were waited for; matrix products, arithmetic and copies ran while one was open for 0% of the time, Pallas kernels for 11%

commit v1 on v0

--- a/solution.py
+++ b/solution.py
@@ -14,6 +14,7 @@
 EZ, EY, EX = CZ + 2 * OV, CY + 2 * OV, CX + 2 * OV
 UZ, UY, UX = CZ + 12, 48, 256
 GROUP = 4
+PIECES = 4
 TABLES = 7
 CHUNK = 2
 INNER = [(z, 4) for z in range(10, 46, 4)]
@@ -705,7 +706,9 @@
     return sigma
 
 
-def combine_kernel(sums, rhs, u0, u1, u2, w0, w1, w2, answer, rest):
+def combine_kernel(
+    sums, rhs, u0, u1, u2, w0, w1, w2, answer_out, rest_out, answer, rest, done
+):
     picked = [
         jnp.sum(jnp.where(lanes()[:1] == i, sums[:1], 0.0), axis=1, keepdims=True)
         for i in range(ITERS * (ITERS + 3) // 2)
@@ -723,19 +726,31 @@
         rest[z] = rhs[z] - (s[0] * w0[z] + s[1] * w1[z] + s[2] * w2[z])
         return carry
 
-    lax.fori_loop(0, CZ, step, 0, unroll=4)
+    layers, copies = CZ // PIECES, []
+    for k in range(PIECES):
+        lax.fori_loop(k * layers, (k + 1) * layers, step, 0, unroll=4)
+        part = pl.ds(k * layers, layers)
+        for i, (source, target) in enumerate(((answer, answer_out), (rest, rest_out))):
+            copies.append(
+                pltpu.make_async_copy(source.at[part], target.at[part], done.at[i, k])
+            )
+            copies[-1].start()
+    for copy in copies:
+        copy.wait()
 
 
 VMEM = pl.BlockSpec(memory_space=pltpu.VMEM)
-
-
-def call(kernel, shapes, operands, scratch=(), cost=2.0):
+HBM = pl.BlockSpec(memory_space=pl.ANY)
+
+
+def call(kernel, shapes, operands, scratch=(), cost=2.0, outside=False):
     return pl.pallas_call(
         kernel,
         out_shape=[jax.ShapeDtypeStruct(shape, f32) for shape in shapes],
         in_specs=[VMEM] * len(operands),
-        out_specs=[VMEM] * len(shapes),
-        scratch_shapes=[pltpu.VMEM(shape, f32) for shape in scratch],
+        out_specs=[HBM if outside else VMEM] * len(shapes),
+        scratch_shapes=[pltpu.VMEM(shape, f32) for shape in scratch]
+        + ([pltpu.SemaphoreType.DMA((2, PIECES))] if outside else []),
         cost_estimate=pl.CostEstimate(
             flops=int(cost * 1e9), bytes_accessed=int(cost * 3.6e6), transcendentals=0
         ),
@@ -859,7 +874,7 @@
         image.append(core)
         sums.append(part)
     operands = [total(sums[-1]), rhs_field, *smooth, *image]
-    return tuple(call(combine_kernel, [CORE] * 2, operands))
+    return tuple(call(combine_kernel, [CORE] * 2, operands, [CORE] * 2, outside=True))
 
 
 def solution(mesh):

time: 170 us -> 170 us (level)
  no operation moved by 1% of the time
where the time goes in v1:
time: 170 us; the launch traced here: 167 us
  starting transfers between devices  75.2 us (44%)
  Pallas kernels  44.7 us (26%)
  waiting for transfers between devices  43.3 us (25%)
  local copies, waits for them, and re-layouts  2.32 us (1%)
    ppermute x32, starting transfers between devices, shifted(): lax.ppermute(block, axis, [(i, (i + step) % count) for i in range(count)])  63.4 us
    pallas_call x25, Pallas kernels, call(): pl.pallas_call(kernel, out_shape=[jax.ShapeDtypeStruct(shape, f32) for sh...  44.7 us
    ppermute x32, waiting for transfers between devices, shifted(): lax.ppermute(block, axis, [(i, (i + step) % count) for i in range(count)])  29.3 us
    ppermute x10, waiting for transfers between devices, ring(): parts.append(lax.ppermute(values, axes, route))  14 us
    ppermute x10, starting transfers between devices, ring(): parts.append(lax.ppermute(values, axes, route))  11.8 us
  transfers between devices with their start and end apart: 42, of which 30 were waited for; matrix products, arithmetic and copies ran while one was open for 0% of the time, Pallas kernels for 11%

profile of v1, /device:TPU:0, one launch (start us, length us, event | category | flops | bytes accessed | tf_op | source)
XLA Modules:
  0.0 166.7 jit_solution(7264209684876617156)
XLA Ops:
  0.6 1.1 copy-done
  1.8 1.1 copy-done.1
  2.9 0.9 shard_map.140
  3.8 4.0 %collective-permute-start = (f32[16,8,128]{2,1,0:T(8,128)S(1)}, f32[16,8,128]{2,1,0:T(8,128)S(1)}, u32[]{:S(2)}, u32[]{:S(2)}) collective-permute-start(f32[16,8,128]{2,1,0:T(8,128)S(1)} %get-tuple-element.67), channel_id=1, source_target_pairs={{0,16},{16,32},{32,48},{48,64},{64,80},{80,96},{96,112},{112,0},{1... | collective-permute-start | bytes 196616 | tf_op jit(solution)/shard_map/ppermute | solution.py:763
  7.8 2.3 %collective-permute-start.1 = (f32[16,8,128]{2,1,0:T(8,128)S(1)}, f32[16,8,128]{2,1,0:T(8,128)S(1)}, u32[]{:S(2)}, u32[]{:S(2)}) collective-permute-start(f32[16,8,128]{2,1,0:T(8,128)S(1)} %get-tuple-element.68), channel_id=1, source_target_pairs={{0,112},{16,0},{32,16},{48,32},{64,48},{80,64},{96,80},{112,96},{1... | collective-permute-start | bytes 196616 | tf_op jit(solution)/shard_map/ppermute | solution.py:763
  10.3 1.7 %collective-permute-start.3 = (f32[54,8,128]{2,1,0:T(8,128)S(1)}, f32[54,8,128]{2,1,0:T(8,128)S(1)}, u32[]{:S(2)}, u32[]{:S(2)}) collective-permute-start(f32[54,8,128]{2,1,0:T(8,128)S(1)} %get-tuple-element.70), channel_id=1, source_target_pairs={{0,12},{4,0},{8,4},{12,8},{1,13},{5,1},{9,5},{13,9},{2,14},{6,2},{... | collective-permute-start | bytes 663560 | tf_op jit(solution)/shard_map/ppermute | solution.py:763
  12.3 1.2 collective-permute-done.1.from_right
  13.7 1.8 %collective-permute-start.5 = (f32[8,8,128]{2,1,0:T(8,128)S(1)}, f32[8,8,128]{2,1,0:T(8,128)S(1)}, u32[]{:S(2)}, u32[]{:S(2)}) collective-permute-start(f32[8,8,128]{2,1,0:T(8,128)S(1)} %get-tuple-element.72), channel_id=1, source_target_pairs={{0,12},{4,0},{8,4},{12,8},{1,13},{5,1},{9,5},{13,9},{2,14},{6,2},{... | collective-permute-start | bytes 98312 | tf_op jit(solution)/shard_map/ppermute | solution.py:763
  15.4 1.9 %collective-permute-done.4.corner_near = f32[8,8,128]{2,1,0:T(8,128)S(1)} collective-permute-done((f32[8,8,128]{2,1,0:T(8,128)S(1)}, f32[8,8,128]{2,1,0:T(8,128)S(1)}, u32[]{:S(2)}, u32[]{:S(2)}) %collective-permute-start.4) | collective-permute-done | bytes 32800 | tf_op jit(solution)/shard_map/ppermute | solution.py:763
  17.6 1.5 shard_map.143
  19.1 1.6 collective-permute-start.6
  20.7 1.7 collective-permute-start.7
  22.4 3.0 %shard_map.144 = (f32[2240,128]{1,0:T(8,128)S(1)}, f32[2240,128]{1,0:T(8,128)S(1)}) custom-call(f32[48,40,256]{2,1,0:T(8,128)S(1)} %get-tuple-element.76.wide, bf16[256,256]{1,0:T(8,128)(2,1)S(1)} %copy-done.7, bf16[256,256]{1,0:T(8,128)(2,1)S(1)} %copy-done.6, bf16[256,256]{1,0:T(8,128)(2,1)S(1)} %copy-done.5, bf16[256,256]{1,0:T(8,128)(2,1)S(1)} %copy-done.4, ...), custom_call_target="tpu_custom_call" | custom-call | flops 4000000000 | bytes 14400000 | tf_op jit(solution)/shard_map/pallas_call | solution.py:747
  25.4 3.4 %collective-permute-done.6.from_below = f32[10,48,128]{2,1,0:T(8,128)S(1)} collective-permute-done((f32[10,48,128]{2,1,0:T(8,128)S(1)}, f32[10,48,128]{2,1,0:T(8,128)S(1)}, u32[]{:S(2)}, u32[]{:S(2)}) %collective-permute-start.6) | collective-permute-done | bytes 245792 | tf_op jit(solution)/shard_map/ppermute | solution.py:763
  29.5 5.0 %shard_map.145 = (f32[56,40,256]{2,1,0:T(8,128)S(1)}, f32[60,48,256]{2,1,0:T(8,128)S(1)}, f32[25,8,128]{2,1,0:T(8,128)S(1)}, f32[25,8,128]{2,1,0:T(8,128)S(1)}) custom-call(f32[10,48,128]{2,1,0:T(8,128)S(1)} %collective-permute-done.6.from_below, f32[10,48,128]{2,1,0:T(8,128)S(1)} %collective-permute-done.7.from_above, ...), custom_call_target="tpu_custom_call" | custom-call | flops 6000000000 | bytes 21600000 | tf_op jit(solution)/shard_map/pallas_call | solution.py:747
  34.5 1.8 %collective-permute-start.8 = (f32[25,8,128]{2,1,0:T(8,128)S(1)}, f32[25,8,128]{2,1,0:T(8,128)S(1)}, u32[]{:S(2)}, u32[]{:S(2)}) collective-permute-start(f32[25,8,128]{2,1,0:T(8,128)S(1)} %get-tuple-element.80), channel_id=1, source_target_pairs={{0,16},{16,32},{32,48},{48,64},{64,80},{80,96},{96,112},{112,0},{1... | collective-permute-start | bytes 307208 | tf_op jit(solution)/shard_map/ppermute | solution.py:763
  36.3 4.2 %collective-permute-start.9 = (f32[25,8,128]{2,1,0:T(8,128)S(1)}, f32[25,8,128]{2,1,0:T(8,128)S(1)}, u32[]{:S(2)}, u32[]{:S(2)}) collective-permute-start(f32[25,8,128]{2,1,0:T(8,128)S(1)} %get-tuple-element.81), channel_id=1, source_target_pairs={{0,112},{16,0},{32,16},{48,32},{64,48},{80,64},{96,80},{112,96},{1... | collective-permute-start | bytes 307208 | tf_op jit(solution)/shard_map/ppermute | solution.py:763
  40.9 1.7 %collective-permute-start.11 = (f32[75,8,128]{2,1,0:T(8,128)S(1)}, f32[75,8,128]{2,1,0:T(8,128)S(1)}, u32[]{:S(2)}, u32[]{:S(2)}) collective-permute-start(f32[75,8,128]{2,1,0:T(8,128)S(1)} %get-tuple-element.83), channel_id=1, source_target_pairs={{0,12},{4,0},{8,4},{12,8},{1,13},{5,1},{9,5},{13,9},{2,14},{6,2},{... | collective-permute-start | bytes 921608 | tf_op jit(solution)/shard_map/ppermute | solution.py:763
  43.2 2.2 %collective-permute-done.9.from_right = f32[25,8,128]{2,1,0:T(8,128)S(1)} collective-permute-done((f32[25,8,128]{2,1,0:T(8,128)S(1)}, f32[25,8,128]{2,1,0:T(8,128)S(1)}, u32[]{:S(2)}, u32[]{:S(2)}) %collective-permute-start.9) | collective-permute-done | bytes 102432 | tf_op jit(solution)/shard_map/ppermute | solution.py:763
  45.5 1.7 %collective-permute-start.13 = (f32[13,8,128]{2,1,0:T(8,128)S(1)}, f32[13,8,128]{2,1,0:T(8,128)S(1)}, u32[]{:S(2)}, u32[]{:S(2)}) collective-permute-start(f32[13,8,128]{2,1,0:T(8,128)S(1)} %get-tuple-element.85), channel_id=1, source_target_pairs={{0,12},{4,0},{8,4},{12,8},{1,13},{5,1},{9,5},{13,9},{2,14},{6,2},{... | collective-permute-start | bytes 159752 | tf_op jit(solution)/shard_map/ppermute | solution.py:763
  47.9 2.2 %collective-permute-done.12.corner_near = f32[13,8,128]{2,1,0:T(8,128)S(1)} collective-permute-done((f32[13,8,128]{2,1,0:T(8,128)S(1)}, f32[13,8,128]{2,1,0:T(8,128)S(1)}, u32[]{:S(2)}, u32[]{:S(2)}) %collective-permute-start.12) | collective-permute-done | bytes 53280 | tf_op jit(solution)/shard_map/ppermute | solution.py:763
  50.2 0.9 shard_map.149
  51.1 1.7 %collective-permute-start.14 = (f32[11,48,128]{2,1,0:T(8,128)S(1)}, f32[11,48,128]{2,1,0:T(8,128)S(1)}, u32[]{:S(2)}, u32[]{:S(2)}) collective-permute-start(f32[11,48,128]{2,1,0:T(8,128)S(1)} %get-tuple-element.87), channel_id=1, source_target_pairs={{0,1},{1,2},{2,3},{3,0},{4,5},{5,6},{6,7},{7,4},{8,9},{9,10},{10,1... | collective-permute-start | bytes 811016 | tf_op jit(solution)/shard_map/ppermute | solution.py:763
  52.8 1.6 collective-permute-start.15
  54.4 5.0 %shard_map.150 = (f32[48,32,128]{2,1,0:T(8,128)S(1)}, f32[48,32,128]{2,1,0:T(8,128)S(1)}, f32[2,8,128]{2,1,0:T(8,128)S(1)}, f32[2240,128]{1,0:T(8,128)S(1)}, f32[2240,128]{1,0:T(8,128)S(1)}) custom-call(f32[56,48,256]{2,1,0:T(8,128)S(1)} %get-tuple-element.86.refs_0_, f32[60,48,256]{2,1,0:T(8,128)S(1)} %get-tuple-element.89.refs_1_.refs_3_, ...), custom_call_target="tpu_custom_call" | custom-call | flops 6000000000 | bytes 21600000 | tf_op jit(solution)/shard_map/pallas_call | solution.py:747
  59.4 2.2 %collective-permute-done.14.refs_1_ = f32[11,48,128]{2,1,0:T(8,128)S(1)} collective-permute-done((f32[11,48,128]{2,1,0:T(8,128)S(1)}, f32[11,48,128]{2,1,0:T(8,128)S(1)}, u32[]{:S(2)}, u32[]{:S(2)}) %collective-permute-start.14) | collective-permute-done | bytes 270368 | tf_op jit(solution)/shard_map/ppermute | solution.py:763
  62.1 7.0 %shard_map.151 = (f32[48,32,128]{2,1,0:T(8,128)S(1)}, f32[48,32,128]{2,1,0:T(8,128)S(1)}, f32[2,8,128]{2,1,0:T(8,128)S(1)}, f32[56,40,256]{2,1,0:T(8,128)S(1)}, ...) custom-call(f32[56,48,256]{2,1,0:T(8,128)S(1)} %get-tuple-element.86.refs_0_, ...), custom_call_target="tpu_custom_call" | custom-call | flops 8000000000 | bytes 28800000 | tf_op jit(solution)/shard_map/pallas_call | solution.py:747
  69.1 13.6 %collective-permute-start.16 = (f32[25,8,128]{2,1,0:T(8,128)S(1)}, f32[25,8,128]{2,1,0:T(8,128)S(1)}, u32[]{:S(2)}, u32[]{:S(2)}) collective-permute-start(f32[25,8,128]{2,1,0:T(8,128)S(1)} %get-tuple-element.96), channel_id=1, source_target_pairs={{0,16},{16,32},{32,48},{48,64},{64,80},{80,96},{96,112},{112,0},{1... | collective-permute-start | bytes 307208 | tf_op jit(solution)/shard_map/ppermute | solution.py:763
  82.7 3.9 %collective-permute-start.17 = (f32[25,8,128]{2,1,0:T(8,128)S(1)}, f32[25,8,128]{2,1,0:T(8,128)S(1)}, u32[]{:S(2)}, u32[]{:S(2)}) collective-permute-start(f32[25,8,128]{2,1,0:T(8,128)S(1)} %get-tuple-element.97), channel_id=1, source_target_pairs={{0,112},{16,0},{32,16},{48,32},{64,48},{80,64},{96,80},{112,96},{1... | collective-permute-start | bytes 307208 | tf_op jit(solution)/shard_map/ppermute | solution.py:763
  86.9 1.7 %collective-permute-start.19 = (f32[75,8,128]{2,1,0:T(8,128)S(1)}, f32[75,8,128]{2,1,0:T(8,128)S(1)}, u32[]{:S(2)}, u32[]{:S(2)}) collective-permute-start(f32[75,8,128]{2,1,0:T(8,128)S(1)} %get-tuple-element.99), channel_id=1, source_target_pairs={{0,12},{4,0},{8,4},{12,8},{1,13},{5,1},{9,5},{13,9},{2,14},{6,2},{... | collective-permute-start | bytes 921608 | tf_op jit(solution)/shard_map/ppermute | solution.py:763
  88.7 0.8 collective-permute-done.16.from_left
  89.5 2.2 %collective-permute-done.17.from_right = f32[25,8,128]{2,1,0:T(8,128)S(1)} collective-permute-done((f32[25,8,128]{2,1,0:T(8,128)S(1)}, f32[25,8,128]{2,1,0:T(8,128)S(1)}, u32[]{:S(2)}, u32[]{:S(2)}) %collective-permute-start.17) | collective-permute-done | bytes 102432 | tf_op jit(solution)/shard_map/ppermute | solution.py:763
  91.8 1.7 %collective-permute-start.21 = (f32[13,8,128]{2,1,0:T(8,128)S(1)}, f32[13,8,128]{2,1,0:T(8,128)S(1)}, u32[]{:S(2)}, u32[]{:S(2)}) collective-permute-start(f32[13,8,128]{2,1,0:T(8,128)S(1)} %get-tuple-element.101), channel_id=1, source_target_pairs={{0,12},{4,0},{8,4},{12,8},{1,13},{5,1},{9,5},{13,9},{2,14},{6,2},{... | collective-permute-start | bytes 159752 | tf_op jit(solution)/shard_map/ppermute | solution.py:763
  94.2 1.9 %collective-permute-done.20.corner_near = f32[13,8,128]{2,1,0:T(8,128)S(1)} collective-permute-done((f32[13,8,128]{2,1,0:T(8,128)S(1)}, f32[13,8,128]{2,1,0:T(8,128)S(1)}, u32[]{:S(2)}, u32[]{:S(2)}) %collective-permute-start.20) | collective-permute-done | bytes 53280 | tf_op jit(solution)/shard_map/ppermute | solution.py:763
  96.3 0.9 shard_map.155
  97.2 1.3 collective-permute-start.22
  98.6 2.0 %collective-permute-start.23 = (f32[11,48,128]{2,1,0:T(8,128)S(1)}, f32[11,48,128]{2,1,0:T(8,128)S(1)}, u32[]{:S(2)}, u32[]{:S(2)}) collective-permute-start(f32[11,48,128]{2,1,0:T(8,128)S(1)} %get-tuple-element.104), channel_id=1, source_target_pairs={{0,3},{1,0},{2,1},{3,2},{4,7},{5,4},{6,5},{7,6},{8,11},{9,8},{10,9... | collective-permute-start | bytes 811016 | tf_op jit(solution)/shard_map/ppermute | solution.py:763
  100.5 5.0 %shard_map.156 = (f32[48,32,128]{2,1,0:T(8,128)S(1)}, f32[48,32,128]{2,1,0:T(8,128)S(1)}, f32[3,8,128]{2,1,0:T(8,128)S(1)}, f32[2240,128]{1,0:T(8,128)S(1)}, f32[2240,128]{1,0:T(8,128)S(1)}) custom-call(f32[56,48,256]{2,1,0:T(8,128)S(1)} %get-tuple-element.102.refs_0_, f32[60,48,256]{2,1,0:T(8,128)S(1)} %get-tuple-element.89.refs_1_.refs_3_, ...), custom_call_target="tpu_custom_call" | custom-call | flops 6000000000 | bytes 21600000 | tf_op jit(solution)/shard_map/pallas_call | solution.py:747
  105.5 2.1 %collective-permute-done.22.refs_1_ = f32[11,48,128]{2,1,0:T(8,128)S(1)} collective-permute-done((f32[11,48,128]{2,1,0:T(8,128)S(1)}, f32[11,48,128]{2,1,0:T(8,128)S(1)}, u32[]{:S(2)}, u32[]{:S(2)}) %collective-permute-start.22) | collective-permute-done | bytes 270368 | tf_op jit(solution)/shard_map/ppermute | solution.py:763
  107.9 7.0 %shard_map.157 = (f32[48,32,128]{2,1,0:T(8,128)S(1)}, f32[48,32,128]{2,1,0:T(8,128)S(1)}, f32[3,8,128]{2,1,0:T(8,128)S(1)}, f32[56,40,256]{2,1,0:T(8,128)S(1)}, ...) custom-call(f32[56,48,256]{2,1,0:T(8,128)S(1)} %get-tuple-element.102.refs_0_, ...), custom_call_target="tpu_custom_call" | custom-call | flops 8000000000 | bytes 28800000 | tf_op jit(solution)/shard_map/pallas_call | solution.py:747
  114.8 2.5 %collective-permute-start.24 = (f32[20,8,128]{2,1,0:T(8,128)S(1)}, f32[20,8,128]{2,1,0:T(8,128)S(1)}, u32[]{:S(2)}, u32[]{:S(2)}) collective-permute-start(f32[20,8,128]{2,1,0:T(8,128)S(1)} %get-tuple-element.112), channel_id=1, source_target_pairs={{0,16},{16,32},{32,48},{48,64},{64,80},{80,96},{96,112},{112,0},{1... | collective-permute-start | bytes 245768 | tf_op jit(solution)/shard_map/ppermute | solution.py:763
  117.3 3.2 %collective-permute-start.25 = (f32[20,8,128]{2,1,0:T(8,128)S(1)}, f32[20,8,128]{2,1,0:T(8,128)S(1)}, u32[]{:S(2)}, u32[]{:S(2)}) collective-permute-start(f32[20,8,128]{2,1,0:T(8,128)S(1)} %get-tuple-element.113), channel_id=1, source_target_pairs={{0,112},{16,0},{32,16},{48,32},{64,48},{80,64},{96,80},{112,96},{1... | collective-permute-start | bytes 245768 | tf_op jit(solution)/shard_map/ppermute | solution.py:763
  120.8 1.7 %collective-permute-start.27 = (f32[60,8,128]{2,1,0:T(8,128)S(1)}, f32[60,8,128]{2,1,0:T(8,128)S(1)}, u32[]{:S(2)}, u32[]{:S(2)}) collective-permute-start(f32[60,8,128]{2,1,0:T(8,128)S(1)} %get-tuple-element.115), channel_id=1, source_target_pairs={{0,12},{4,0},{8,4},{12,8},{1,13},{5,1},{9,5},{13,9},{2,14},{6,2},{... | collective-permute-start | bytes 737288 | tf_op jit(solution)/shard_map/ppermute | solution.py:763
  123.0 1.7 %collective-permute-done.25.from_right = f32[20,8,128]{2,1,0:T(8,128)S(1)} collective-permute-done((f32[20,8,128]{2,1,0:T(8,128)S(1)}, f32[20,8,128]{2,1,0:T(8,128)S(1)}, u32[]{:S(2)}, u32[]{:S(2)}) %collective-permute-start.25) | collective-permute-done | bytes 81952 | tf_op jit(solution)/shard_map/ppermute | solution.py:763
  124.8 1.7 %collective-permute-start.29 = (f32[8,8,128]{2,1,0:T(8,128)S(1)}, f32[8,8,128]{2,1,0:T(8,128)S(1)}, u32[]{:S(2)}, u32[]{:S(2)}) collective-permute-start(f32[8,8,128]{2,1,0:T(8,128)S(1)} %get-tuple-element.117), channel_id=1, source_target_pairs={{0,12},{4,0},{8,4},{12,8},{1,13},{5,1},{9,5},{13,9},{2,14},{6,2},{... | collective-permute-start | bytes 98312 | tf_op jit(solution)/shard_map/ppermute | solution.py:763
  127.2 1.3 collective-permute-done.28.corner_near
  128.6 0.7 shard_map.161
  129.3 1.5 collective-permute-start.30
  130.8 2.1 %collective-permute-start.31 = (f32[7,48,128]{2,1,0:T(8,128)S(1)}, f32[7,48,128]{2,1,0:T(8,128)S(1)}, u32[]{:S(2)}, u32[]{:S(2)}) collective-permute-start(f32[7,48,128]{2,1,0:T(8,128)S(1)} %get-tuple-element.120), channel_id=1, source_target_pairs={{0,3},{1,0},{2,1},{3,2},{4,7},{5,4},{6,5},{7,6},{8,11},{9,8},{10,9... | collective-permute-start | bytes 516104 | tf_op jit(solution)/shard_map/ppermute | solution.py:763
  132.9 2.2 %shard_map.162 = (f32[48,32,128]{2,1,0:T(8,128)S(1)}, f32[48,32,128]{2,1,0:T(8,128)S(1)}, f32[4,8,128]{2,1,0:T(8,128)S(1)}) custom-call(f32[56,48,256]{2,1,0:T(8,128)S(1)} %get-tuple-element.118.refs_0_, f32[60,48,256]{2,1,0:T(8,128)S(1)} %get-tuple-element.89.refs_1_.refs_3_, f32[48,32,128]{2,1,0:T(8,128)S(1)} %copy-done.2, ...), custom_call_target="tpu_custom_call" | custom-call | flops 6000000000 | bytes 21600000 | tf_op jit(solution)/shard_map/pallas_call | solution.py:747
  135.1 2.5 %collective-permute-done.30.refs_1_ = f32[7,48,128]{2,1,0:T(8,128)S(1)} collective-permute-done((f32[7,48,128]{2,1,0:T(8,128)S(1)}, f32[7,48,128]{2,1,0:T(8,128)S(1)}, u32[]{:S(2)}, u32[]{:S(2)}) %collective-permute-start.30) | collective-permute-done | bytes 172064 | tf_op jit(solution)/shard_map/ppermute | solution.py:763
  137.9 1.3 shard_map.163
  139.2 1.2 collective-permute-done.32
  140.4 1.6 collective-permute-start.35
  142.0 1.8 %collective-permute-start.34 = (f32[8,128]{1,0:T(8,128)S(1)}, f32[8,128]{1,0:T(8,128)S(1)}, u32[]{:S(2)}, u32[]{:S(2)}) collective-permute-start(f32[8,128]{1,0:T(8,128)S(1)} %add.30), channel_id=1, source_target_pairs={{0,16},{4,20},{8,24},{12,28},{16,0},{20,4},{24,8},{28,12},{32,48},... | collective-permute-start | bytes 12296 | tf_op jit(solution)/shard_map/ppermute | solution.py:777
  144.0 3.1 %collective-permute-done.34 = f32[8,128]{1,0:T(8,128)S(1)} collective-permute-done((f32[8,128]{1,0:T(8,128)S(1)}, f32[8,128]{1,0:T(8,128)S(1)}, u32[]{:S(2)}, u32[]{:S(2)}) %collective-permute-start.34) | collective-permute-done | bytes 4128 | tf_op jit(solution)/shard_map/ppermute | solution.py:777
  147.1 1.6 collective-permute-done.33
  148.7 2.8 %collective-permute-start.38 = (f32[8,128]{1,0:T(8,128)S(1)}, f32[8,128]{1,0:T(8,128)S(1)}, u32[]{:S(2)}, u32[]{:S(2)}) collective-permute-start(f32[8,128]{1,0:T(8,128)S(1)} %add_add_fusion.2), channel_id=1, source_target_pairs={{0,96},{16,112},{32,0},{48,16},{64,32},{80,48},{96,64},{112,80},{1... | collective-permute-start | bytes 12296 | tf_op jit(solution)/shard_map/ppermute | solution.py:777
  151.5 0.9 collective-permute-start.36
  152.8 3.8 %collective-permute-done.37 = f32[8,128]{1,0:T(8,128)S(1)} collective-permute-done((f32[8,128]{1,0:T(8,128)S(1)}, f32[8,128]{1,0:T(8,128)S(1)}, u32[]{:S(2)}, u32[]{:S(2)}) %collective-permute-start.37) | collective-permute-done | bytes 4128 | tf_op jit(solution)/shard_map/ppermute | solution.py:777
  156.6 3.3 %collective-permute-start.41 = (f32[8,128]{1,0:T(8,128)S(1)}, f32[8,128]{1,0:T(8,128)S(1)}, u32[]{:S(2)}, u32[]{:S(2)}) collective-permute-start(f32[8,128]{1,0:T(8,128)S(1)} %add_add_fusion.1), channel_id=1, source_target_pairs={{0,3},{1,0},{2,1},{3,2},{4,7},{5,4},{6,5},{7,6},{8,11},{9,8},{10,9... | collective-permute-start | bytes 12296 | tf_op jit(solution)/shard_map/ppermute | solution.py:777
  160.2 1.0 collective-permute-start.39
  161.2 3.8 %collective-permute-done.40 = f32[8,128]{1,0:T(8,128)S(1)} collective-permute-done((f32[8,128]{1,0:T(8,128)S(1)}, f32[8,128]{1,0:T(8,128)S(1)}, u32[]{:S(2)}, u32[]{:S(2)}) %collective-permute-start.40) | collective-permute-done | bytes 4128 | tf_op jit(solution)/shard_map/ppermute | solution.py:777
  165.0 1.4 shard_map.164
  (71 shorter events, 8.1 us)
Async XLA Ops:
  0.6 1.1 copy-start
  1.8 1.1 copy-start.1
  3.8 8.6 %collective-permute-start = (f32[16,8,128]{2,1,0:T(8,128)S(1)}, f32[16,8,128]{2,1,0:T(8,128)S(1)}, u32[]{:S(2)}, u32[]{:S(2)}) collective-permute-start(f32[16,8,128]{2,1,0:T(8,128)S(1)} %get-tuple-element.67), channel_id=1, source_target_pairs={{0,16},{16,32},{32,48},{48,64},{64,80},{80,96},{96,112},{112,0},{1... | collective-permute-start | bytes 196616 | tf_op jit(solution)/shard_map/ppermute | solution.py:763
  7.8 5.8 %collective-permute-start.1 = (f32[16,8,128]{2,1,0:T(8,128)S(1)}, f32[16,8,128]{2,1,0:T(8,128)S(1)}, u32[]{:S(2)}, u32[]{:S(2)}) collective-permute-start(f32[16,8,128]{2,1,0:T(8,128)S(1)} %get-tuple-element.68), channel_id=1, source_target_pairs={{0,112},{16,0},{32,16},{48,32},{64,48},{80,64},{96,80},{112,96},{1... | collective-permute-start | bytes 196616 | tf_op jit(solution)/shard_map/ppermute | solution.py:763
  10.2 7.4 %collective-permute-start.2 = (f32[54,8,128]{2,1,0:T(8,128)S(1)}, f32[54,8,128]{2,1,0:T(8,128)S(1)}, u32[]{:S(2)}, u32[]{:S(2)}) collective-permute-start(f32[54,8,128]{2,1,0:T(8,128)S(1)} %get-tuple-element.69), channel_id=1, source_target_pairs={{0,4},{4,8},{8,12},{12,0},{1,5},{5,9},{9,13},{13,1},{2,6},{6,10},{... | collective-permute-start | bytes 663560 | tf_op jit(solution)/shard_map/ppermute | solution.py:763
  10.3 7.3 %copy-start.2 = (f32[48,32,128]{2,1,0:T(8,128)S(1)}, f32[48,32,128]{2,1,0:T(8,128)}, u32[]{:S(2)}) copy-start(f32[48,32,128]{2,1,0:T(8,128)} %rhs.7) | copy-start | bytes 2359300
  10.3 7.3 %collective-permute-start.3 = (f32[54,8,128]{2,1,0:T(8,128)S(1)}, f32[54,8,128]{2,1,0:T(8,128)S(1)}, u32[]{:S(2)}, u32[]{:S(2)}) collective-permute-start(f32[54,8,128]{2,1,0:T(8,128)S(1)} %get-tuple-element.70), channel_id=1, source_target_pairs={{0,12},{4,0},{8,4},{12,8},{1,13},{5,1},{9,5},{13,9},{2,14},{6,2},{... | collective-permute-start | bytes 663560 | tf_op jit(solution)/shard_map/ppermute | solution.py:763
  13.6 3.7 %collective-permute-start.4 = (f32[8,8,128]{2,1,0:T(8,128)S(1)}, f32[8,8,128]{2,1,0:T(8,128)S(1)}, u32[]{:S(2)}, u32[]{:S(2)}) collective-permute-start(f32[8,8,128]{2,1,0:T(8,128)S(1)} %get-tuple-element.71), channel_id=1, source_target_pairs={{0,4},{4,8},{8,12},{12,0},{1,5},{5,9},{9,13},{13,1},{2,6},{6,10},{... | collective-permute-start | bytes 98312 | tf_op jit(solution)/shard_map/ppermute | solution.py:763
  13.6 8.8 %copy-start.4 = (bf16[256,256]{1,0:T(8,128)(2,1)S(1)}, bf16[256,256]{1,0:T(8,128)(2,1)}, u32[]{:S(2)}) copy-start(bf16[256,256]{1,0:T(8,128)(2,1)} %constant.25.clone.refs_3_.refs_6_.refs_14_.refs_7_.refs_15_) | copy-start | bytes 393220
  13.6 8.8 %copy-start.5 = (bf16[256,256]{1,0:T(8,128)(2,1)S(1)}, bf16[256,256]{1,0:T(8,128)(2,1)}, u32[]{:S(2)}) copy-start(bf16[256,256]{1,0:T(8,128)(2,1)} %constant.24.clone.refs_2_.refs_5_.refs_13_.refs_6_.refs_14_) | copy-start | bytes 393220
  13.6 8.8 %copy-start.6 = (bf16[256,256]{1,0:T(8,128)(2,1)S(1)}, bf16[256,256]{1,0:T(8,128)(2,1)}, u32[]{:S(2)}) copy-start(bf16[256,256]{1,0:T(8,128)(2,1)} %constant.23.clone.refs_1_.refs_4_.refs_12_.refs_5_.refs_13_) | copy-start | bytes 393220
  13.6 8.8 %copy-start.7 = (bf16[256,256]{1,0:T(8,128)(2,1)S(1)}, bf16[256,256]{1,0:T(8,128)(2,1)}, u32[]{:S(2)}) copy-start(bf16[256,256]{1,0:T(8,128)(2,1)} %constant.22.clone.refs_0_.refs_3_.refs_11_.refs_4_.refs_12_) | copy-start | bytes 393220
  13.6 8.8 %copy-start.8 = (bf16[80,240]{1,0:T(8,128)(2,1)S(1)}, bf16[80,240]{1,0:T(8,128)(2,1)}, u32[]{:S(2)}) copy-start(bf16[80,240]{1,0:T(8,128)(2,1)} %constant.34.refs_5_.refs_8_.refs_16_.refs_9_.refs_17_) | copy-start | bytes 115204
  13.6 8.8 %copy-start.9 = (bf16[80,240]{1,0:T(8,128)(2,1)S(1)}, bf16[80,240]{1,0:T(8,128)(2,1)}, u32[]{:S(2)}) copy-start(bf16[80,240]{1,0:T(8,128)(2,1)} %constant.33.refs_4_.refs_7_.refs_15_.refs_8_.refs_16_) | copy-start | bytes 115204
  13.6 8.8 %copy-start.10 = (bf16[56,168]{1,0:T(8,128)(2,1)S(1)}, bf16[56,168]{1,0:T(8,128)(2,1)}, u32[]{:S(2)}) copy-start(bf16[56,168]{1,0:T(8,128)(2,1)} %constant.35.refs_6_.refs_9_.refs_17_.refs_10_.refs_18_) | copy-start | bytes 56452
  13.7 3.9 %collective-permute-start.5 = (f32[8,8,128]{2,1,0:T(8,128)S(1)}, f32[8,8,128]{2,1,0:T(8,128)S(1)}, u32[]{:S(2)}, u32[]{:S(2)}) collective-permute-start(f32[8,8,128]{2,1,0:T(8,128)S(1)} %get-tuple-element.72), channel_id=1, source_target_pairs={{0,12},{4,0},{8,4},{12,8},{1,13},{5,1},{9,5},{13,9},{2,14},{6,2},{... | collective-permute-start | bytes 98312 | tf_op jit(solution)/shard_map/ppermute | solution.py:763
  19.1 9.8 %collective-permute-start.6 = (f32[10,48,128]{2,1,0:T(8,128)S(1)}, f32[10,48,128]{2,1,0:T(8,128)S(1)}, u32[]{:S(2)}, u32[]{:S(2)}) collective-permute-start(f32[10,48,128]{2,1,0:T(8,128)S(1)} %get-tuple-element.73), channel_id=1, source_target_pairs={{0,1},{1,2},{2,3},{3,0},{4,5},{5,6},{6,7},{7,4},{8,9},{9,10},{10,1... | collective-permute-start | bytes 737288 | tf_op jit(solution)/shard_map/ppermute | solution.py:763
  20.7 8.8 %collective-permute-start.7 = (f32[10,48,128]{2,1,0:T(8,128)S(1)}, f32[10,48,128]{2,1,0:T(8,128)S(1)}, u32[]{:S(2)}, u32[]{:S(2)}) collective-permute-start(f32[10,48,128]{2,1,0:T(8,128)S(1)} %get-tuple-element.74), channel_id=1, source_target_pairs={{0,3},{1,0},{2,1},{3,2},{4,7},{5,4},{6,5},{7,6},{8,11},{9,8},{10,9... | collective-permute-start | bytes 737288 | tf_op jit(solution)/shard_map/ppermute | solution.py:763
  22.4 7.1 %copy-start.3 = (f32[40,56,256]{2,1,0:T(8,128)S(1)}, f32[40,56,256]{2,1,0:T(8,128)}, u32[]{:S(2)}) copy-start(f32[40,56,256]{2,1,0:T(8,128)} %constant.32.clone.refs_2_.refs_10_.refs_11_) | copy-start | bytes 6881284
  34.5 8.7 %collective-permute-start.8 = (f32[25,8,128]{2,1,0:T(8,128)S(1)}, f32[25,8,128]{2,1,0:T(8,128)S(1)}, u32[]{:S(2)}, u32[]{:S(2)}) collective-permute-start(f32[25,8,128]{2,1,0:T(8,128)S(1)} %get-tuple-element.80), channel_id=1, source_target_pairs={{0,16},{16,32},{32,48},{48,64},{64,80},{80,96},{96,112},{112,0},{1... | collective-permute-start | bytes 307208 | tf_op jit(solution)/shard_map/ppermute | solution.py:763
  36.3 9.1 %collective-permute-start.9 = (f32[25,8,128]{2,1,0:T(8,128)S(1)}, f32[25,8,128]{2,1,0:T(8,128)S(1)}, u32[]{:S(2)}, u32[]{:S(2)}) collective-permute-start(f32[25,8,128]{2,1,0:T(8,128)S(1)} %get-tuple-element.81), channel_id=1, source_target_pairs={{0,112},{16,0},{32,16},{48,32},{64,48},{80,64},{96,80},{112,96},{1... | collective-permute-start | bytes 307208 | tf_op jit(solution)/shard_map/ppermute | solution.py:763
  40.8 9.4 %collective-permute-start.10 = (f32[75,8,128]{2,1,0:T(8,128)S(1)}, f32[75,8,128]{2,1,0:T(8,128)S(1)}, u32[]{:S(2)}, u32[]{:S(2)}) collective-permute-start(f32[75,8,128]{2,1,0:T(8,128)S(1)} %get-tuple-element.82), channel_id=1, source_target_pairs={{0,4},{4,8},{8,12},{12,0},{1,5},{5,9},{9,13},{13,1},{2,6},{6,10},{... | collective-permute-start | bytes 921608 | tf_op jit(solution)/shard_map/ppermute | solution.py:763
  40.9 9.3 %collective-permute-start.11 = (f32[75,8,128]{2,1,0:T(8,128)S(1)}, f32[75,8,128]{2,1,0:T(8,128)S(1)}, u32[]{:S(2)}, u32[]{:S(2)}) collective-permute-start(f32[75,8,128]{2,1,0:T(8,128)S(1)} %get-tuple-element.83), channel_id=1, source_target_pairs={{0,12},{4,0},{8,4},{12,8},{1,13},{5,1},{9,5},{13,9},{2,14},{6,2},{... | collective-permute-start | bytes 921608 | tf_op jit(solution)/shard_map/ppermute | solution.py:763
  45.4 4.7 %collective-permute-start.12 = (f32[13,8,128]{2,1,0:T(8,128)S(1)}, f32[13,8,128]{2,1,0:T(8,128)S(1)}, u32[]{:S(2)}, u32[]{:S(2)}) collective-permute-start(f32[13,8,128]{2,1,0:T(8,128)S(1)} %get-tuple-element.84), channel_id=1, source_target_pairs={{0,4},{4,8},{8,12},{12,0},{1,5},{5,9},{9,13},{13,1},{2,6},{6,10},{... | collective-permute-start | bytes 159752 | tf_op jit(solution)/shard_map/ppermute | solution.py:763
  45.5 4.7 %collective-permute-start.13 = (f32[13,8,128]{2,1,0:T(8,128)S(1)}, f32[13,8,128]{2,1,0:T(8,128)S(1)}, u32[]{:S(2)}, u32[]{:S(2)}) collective-permute-start(f32[13,8,128]{2,1,0:T(8,128)S(1)} %get-tuple-element.85), channel_id=1, source_target_pairs={{0,12},{4,0},{8,4},{12,8},{1,13},{5,1},{9,5},{13,9},{2,14},{6,2},{... | collective-permute-start | bytes 159752 | tf_op jit(solution)/shard_map/ppermute | solution.py:763
  51.1 10.4 %collective-permute-start.14 = (f32[11,48,128]{2,1,0:T(8,128)S(1)}, f32[11,48,128]{2,1,0:T(8,128)S(1)}, u32[]{:S(2)}, u32[]{:S(2)}) collective-permute-start(f32[11,48,128]{2,1,0:T(8,128)S(1)} %get-tuple-element.87), channel_id=1, source_target_pairs={{0,1},{1,2},{2,3},{3,0},{4,5},{5,6},{6,7},{7,4},{8,9},{9,10},{10,1... | collective-permute-start | bytes 811016 | tf_op jit(solution)/shard_map/ppermute | solution.py:763
  52.8 9.3 %collective-permute-start.15 = (f32[11,48,128]{2,1,0:T(8,128)S(1)}, f32[11,48,128]{2,1,0:T(8,128)S(1)}, u32[]{:S(2)}, u32[]{:S(2)}) collective-permute-start(f32[11,48,128]{2,1,0:T(8,128)S(1)} %get-tuple-element.88), channel_id=1, source_target_pairs={{0,3},{1,0},{2,1},{3,2},{4,7},{5,4},{6,5},{7,6},{8,11},{9,8},{10,9... | collective-permute-start | bytes 811016 | tf_op jit(solution)/shard_map/ppermute | solution.py:763
  69.1 20.4 %collective-permute-start.16 = (f32[25,8,128]{2,1,0:T(8,128)S(1)}, f32[25,8,128]{2,1,0:T(8,128)S(1)}, u32[]{:S(2)}, u32[]{:S(2)}) collective-permute-start(f32[25,8,128]{2,1,0:T(8,128)S(1)} %get-tuple-element.96), channel_id=1, source_target_pairs={{0,16},{16,32},{32,48},{48,64},{64,80},{80,96},{96,112},{112,0},{1... | collective-permute-start | bytes 307208 | tf_op jit(solution)/shard_map/ppermute | solution.py:763
  82.7 9.0 %collective-permute-start.17 = (f32[25,8,128]{2,1,0:T(8,128)S(1)}, f32[25,8,128]{2,1,0:T(8,128)S(1)}, u32[]{:S(2)}, u32[]{:S(2)}) collective-permute-start(f32[25,8,128]{2,1,0:T(8,128)S(1)} %get-tuple-element.97), channel_id=1, source_target_pairs={{0,112},{16,0},{32,16},{48,32},{64,48},{80,64},{96,80},{112,96},{1... | collective-permute-start | bytes 307208 | tf_op jit(solution)/shard_map/ppermute | solution.py:763
  86.8 9.5 %collective-permute-start.18 = (f32[75,8,128]{2,1,0:T(8,128)S(1)}, f32[75,8,128]{2,1,0:T(8,128)S(1)}, u32[]{:S(2)}, u32[]{:S(2)}) collective-permute-start(f32[75,8,128]{2,1,0:T(8,128)S(1)} %get-tuple-element.98), channel_id=1, source_target_pairs={{0,4},{4,8},{8,12},{12,0},{1,5},{5,9},{9,13},{13,1},{2,6},{6,10},{... | collective-permute-start | bytes 921608 | tf_op jit(solution)/shard_map/ppermute | solution.py:763
  86.9 9.4 %collective-permute-start.19 = (f32[75,8,128]{2,1,0:T(8,128)S(1)}, f32[75,8,128]{2,1,0:T(8,128)S(1)}, u32[]{:S(2)}, u32[]{:S(2)}) collective-permute-start(f32[75,8,128]{2,1,0:T(8,128)S(1)} %get-tuple-element.99), channel_id=1, source_target_pairs={{0,12},{4,0},{8,4},{12,8},{1,13},{5,1},{9,5},{13,9},{2,14},{6,2},{... | collective-permute-start | bytes 921608 | tf_op jit(solution)/shard_map/ppermute | solution.py:763
  91.7 4.4 %collective-permute-start.20 = (f32[13,8,128]{2,1,0:T(8,128)S(1)}, f32[13,8,128]{2,1,0:T(8,128)S(1)}, u32[]{:S(2)}, u32[]{:S(2)}) collective-permute-start(f32[13,8,128]{2,1,0:T(8,128)S(1)} %get-tuple-element.100), channel_id=1, source_target_pairs={{0,4},{4,8},{8,12},{12,0},{1,5},{5,9},{9,13},{13,1},{2,6},{6,10},{... | collective-permute-start | bytes 159752 | tf_op jit(solution)/shard_map/ppermute | solution.py:763
  91.8 4.5 %collective-permute-start.21 = (f32[13,8,128]{2,1,0:T(8,128)S(1)}, f32[13,8,128]{2,1,0:T(8,128)S(1)}, u32[]{:S(2)}, u32[]{:S(2)}) collective-permute-start(f32[13,8,128]{2,1,0:T(8,128)S(1)} %get-tuple-element.101), channel_id=1, source_target_pairs={{0,12},{4,0},{8,4},{12,8},{1,13},{5,1},{9,5},{13,9},{2,14},{6,2},{... | collective-permute-start | bytes 159752 | tf_op jit(solution)/shard_map/ppermute | solution.py:763
  97.2 10.4 %collective-permute-start.22 = (f32[11,48,128]{2,1,0:T(8,128)S(1)}, f32[11,48,128]{2,1,0:T(8,128)S(1)}, u32[]{:S(2)}, u32[]{:S(2)}) collective-permute-start(f32[11,48,128]{2,1,0:T(8,128)S(1)} %get-tuple-element.103), channel_id=1, source_target_pairs={{0,1},{1,2},{2,3},{3,0},{4,5},{5,6},{6,7},{7,4},{8,9},{9,10},{10,1... | collective-permute-start | bytes 811016 | tf_op jit(solution)/shard_map/ppermute | solution.py:763
  98.6 9.3 %collective-permute-start.23 = (f32[11,48,128]{2,1,0:T(8,128)S(1)}, f32[11,48,128]{2,1,0:T(8,128)S(1)}, u32[]{:S(2)}, u32[]{:S(2)}) collective-permute-start(f32[11,48,128]{2,1,0:T(8,128)S(1)} %get-tuple-element.104), channel_id=1, source_target_pairs={{0,3},{1,0},{2,1},{3,2},{4,7},{5,4},{6,5},{7,6},{8,11},{9,8},{10,9... | collective-permute-start | bytes 811016 | tf_op jit(solution)/shard_map/ppermute | solution.py:763
  114.8 8.1 %collective-permute-start.24 = (f32[20,8,128]{2,1,0:T(8,128)S(1)}, f32[20,8,128]{2,1,0:T(8,128)S(1)}, u32[]{:S(2)}, u32[]{:S(2)}) collective-permute-start(f32[20,8,128]{2,1,0:T(8,128)S(1)} %get-tuple-element.112), channel_id=1, source_target_pairs={{0,16},{16,32},{32,48},{48,64},{64,80},{80,96},{96,112},{112,0},{1... | collective-permute-start | bytes 245768 | tf_op jit(solution)/shard_map/ppermute | solution.py:763
  117.3 7.4 %collective-permute-start.25 = (f32[20,8,128]{2,1,0:T(8,128)S(1)}, f32[20,8,128]{2,1,0:T(8,128)S(1)}, u32[]{:S(2)}, u32[]{:S(2)}) collective-permute-start(f32[20,8,128]{2,1,0:T(8,128)S(1)} %get-tuple-element.113), channel_id=1, source_target_pairs={{0,112},{16,0},{32,16},{48,32},{64,48},{80,64},{96,80},{112,96},{1... | collective-permute-start | bytes 245768 | tf_op jit(solution)/shard_map/ppermute | solution.py:763
  120.8 7.8 %collective-permute-start.26 = (f32[60,8,128]{2,1,0:T(8,128)S(1)}, f32[60,8,128]{2,1,0:T(8,128)S(1)}, u32[]{:S(2)}, u32[]{:S(2)}) collective-permute-start(f32[60,8,128]{2,1,0:T(8,128)S(1)} %get-tuple-element.114), channel_id=1, source_target_pairs={{0,4},{4,8},{8,12},{12,0},{1,5},{5,9},{9,13},{13,1},{2,6},{6,10},{... | collective-permute-start | bytes 737288 | tf_op jit(solution)/shard_map/ppermute | solution.py:763
  120.8 7.7 %collective-permute-start.27 = (f32[60,8,128]{2,1,0:T(8,128)S(1)}, f32[60,8,128]{2,1,0:T(8,128)S(1)}, u32[]{:S(2)}, u32[]{:S(2)}) collective-permute-start(f32[60,8,128]{2,1,0:T(8,128)S(1)} %get-tuple-element.115), channel_id=1, source_target_pairs={{0,12},{4,0},{8,4},{12,8},{1,13},{5,1},{9,5},{13,9},{2,14},{6,2},{... | collective-permute-start | bytes 737288 | tf_op jit(solution)/shard_map/ppermute | solution.py:763
  124.7 3.8 %collective-permute-start.28 = (f32[8,8,128]{2,1,0:T(8,128)S(1)}, f32[8,8,128]{2,1,0:T(8,128)S(1)}, u32[]{:S(2)}, u32[]{:S(2)}) collective-permute-start(f32[8,8,128]{2,1,0:T(8,128)S(1)} %get-tuple-element.116), channel_id=1, source_target_pairs={{0,4},{4,8},{8,12},{12,0},{1,5},{5,9},{9,13},{13,1},{2,6},{6,10},{... | collective-permute-start | bytes 98312 | tf_op jit(solution)/shard_map/ppermute | solution.py:763
  124.8 3.7 %collective-permute-start.29 = (f32[8,8,128]{2,1,0:T(8,128)S(1)}, f32[8,8,128]{2,1,0:T(8,128)S(1)}, u32[]{:S(2)}, u32[]{:S(2)}) collective-permute-start(f32[8,8,128]{2,1,0:T(8,128)S(1)} %get-tuple-element.117), channel_id=1, source_target_pairs={{0,12},{4,0},{8,4},{12,8},{1,13},{5,1},{9,5},{13,9},{2,14},{6,2},{... | collective-permute-start | bytes 98312 | tf_op jit(solution)/shard_map/ppermute | solution.py:763
  129.3 8.3 %collective-permute-start.30 = (f32[7,48,128]{2,1,0:T(8,128)S(1)}, f32[7,48,128]{2,1,0:T(8,128)S(1)}, u32[]{:S(2)}, u32[]{:S(2)}) collective-permute-start(f32[7,48,128]{2,1,0:T(8,128)S(1)} %get-tuple-element.119), channel_id=1, source_target_pairs={{0,1},{1,2},{2,3},{3,0},{4,5},{5,6},{6,7},{7,4},{8,9},{9,10},{10,1... | collective-permute-start | bytes 516104 | tf_op jit(solution)/shard_map/ppermute | solution.py:763
  130.8 7.1 %collective-permute-start.31 = (f32[7,48,128]{2,1,0:T(8,128)S(1)}, f32[7,48,128]{2,1,0:T(8,128)S(1)}, u32[]{:S(2)}, u32[]{:S(2)}) collective-permute-start(f32[7,48,128]{2,1,0:T(8,128)S(1)} %get-tuple-element.120), channel_id=1, source_target_pairs={{0,3},{1,0},{2,1},{3,2},{4,7},{5,4},{6,5},{7,6},{8,11},{9,8},{10,9... | collective-permute-start | bytes 516104 | tf_op jit(solution)/shard_map/ppermute | solution.py:763
  139.2 1.2 collective-permute-start.32
  140.4 3.6 %collective-permute-start.35 = (f32[8,128]{1,0:T(8,128)S(1)}, f32[8,128]{1,0:T(8,128)S(1)}, u32[]{:S(2)}, u32[]{:S(2)}) collective-permute-start(f32[8,128]{1,0:T(8,128)S(1)} %add.30), channel_id=1, source_target_pairs={{0,24},{4,28},{8,0},{12,4},{16,8},{20,12},{24,16},{28,20},{32,56},... | collective-permute-start | bytes 12296 | tf_op jit(solution)/shard_map/ppermute | solution.py:777
  142.0 5.1 %collective-permute-start.34 = (f32[8,128]{1,0:T(8,128)S(1)}, f32[8,128]{1,0:T(8,128)S(1)}, u32[]{:S(2)}, u32[]{:S(2)}) collective-permute-start(f32[8,128]{1,0:T(8,128)S(1)} %add.30), channel_id=1, source_target_pairs={{0,16},{4,20},{8,24},{12,28},{16,0},{20,4},{24,8},{28,12},{32,48},... | collective-permute-start | bytes 12296 | tf_op jit(solution)/shard_map/ppermute | solution.py:777
  143.9 4.8 %collective-permute-start.33 = (f32[8,128]{1,0:T(8,128)S(1)}, f32[8,128]{1,0:T(8,128)S(1)}, u32[]{:S(2)}, u32[]{:S(2)}) collective-permute-start(f32[8,128]{1,0:T(8,128)S(1)} %add.30), channel_id=1, source_target_pairs={{0,8},{4,12},{8,16},{12,20},{16,24},{20,28},{24,0},{28,4},{32,40},... | collective-permute-start | bytes 12296 | tf_op jit(solution)/shard_map/ppermute | solution.py:777
  148.7 4.1 %collective-permute-start.38 = (f32[8,128]{1,0:T(8,128)S(1)}, f32[8,128]{1,0:T(8,128)S(1)}, u32[]{:S(2)}, u32[]{:S(2)}) collective-permute-start(f32[8,128]{1,0:T(8,128)S(1)} %add_add_fusion.2), channel_id=1, source_target_pairs={{0,96},{16,112},{32,0},{48,16},{64,32},{80,48},{96,64},{112,80},{1... | collective-permute-start | bytes 12296 | tf_op jit(solution)/shard_map/ppermute | solution.py:777
  151.4 5.1 %collective-permute-start.37 = (f32[8,128]{1,0:T(8,128)S(1)}, f32[8,128]{1,0:T(8,128)S(1)}, u32[]{:S(2)}, u32[]{:S(2)}) collective-permute-start(f32[8,128]{1,0:T(8,128)S(1)} %add_add_fusion.2), channel_id=1, source_target_pairs={{0,64},{16,80},{32,96},{48,112},{64,0},{80,16},{96,32},{112,48},{1... | collective-permute-start | bytes 12296 | tf_op jit(solution)/shard_map/ppermute | solution.py:777
  151.5 5.1 %collective-permute-start.36 = (f32[8,128]{1,0:T(8,128)S(1)}, f32[8,128]{1,0:T(8,128)S(1)}, u32[]{:S(2)}, u32[]{:S(2)}) collective-permute-start(f32[8,128]{1,0:T(8,128)S(1)} %add_add_fusion.2), channel_id=1, source_target_pairs={{0,32},{16,48},{32,64},{48,80},{64,96},{80,112},{96,0},{112,16},{1... | collective-permute-start | bytes 12296 | tf_op jit(solution)/shard_map/ppermute | solution.py:777
  156.6 4.6 %collective-permute-start.41 = (f32[8,128]{1,0:T(8,128)S(1)}, f32[8,128]{1,0:T(8,128)S(1)}, u32[]{:S(2)}, u32[]{:S(2)}) collective-permute-start(f32[8,128]{1,0:T(8,128)S(1)} %add_add_fusion.1), channel_id=1, source_target_pairs={{0,3},{1,0},{2,1},{3,2},{4,7},{5,4},{6,5},{7,6},{8,11},{9,8},{10,9... | collective-permute-start | bytes 12296 | tf_op jit(solution)/shard_map/ppermute | solution.py:777
  159.9 5.1 %collective-permute-start.40 = (f32[8,128]{1,0:T(8,128)S(1)}, f32[8,128]{1,0:T(8,128)S(1)}, u32[]{:S(2)}, u32[]{:S(2)}) collective-permute-start(f32[8,128]{1,0:T(8,128)S(1)} %add_add_fusion.1), channel_id=1, source_target_pairs={{0,2},{1,3},{2,0},{3,1},{4,6},{5,7},{6,4},{7,5},{8,10},{9,11},{10,... | collective-permute-start | bytes 12296 | tf_op jit(solution)/shard_map/ppermute | solution.py:777
  160.2 4.8 %collective-permute-start.39 = (f32[8,128]{1,0:T(8,128)S(1)}, f32[8,128]{1,0:T(8,128)S(1)}, u32[]{:S(2)}, u32[]{:S(2)}) collective-permute-start(f32[8,128]{1,0:T(8,128)S(1)} %add_add_fusion.1), channel_id=1, source_target_pairs={{0,1},{1,2},{2,3},{3,0},{4,5},{5,6},{6,7},{7,4},{8,9},{9,10},{10,1... | collective-permute-start | bytes 12296 | tf_op jit(solution)/shard_map/ppermute | solution.py:777
